TPU v7x, 32 devices: a whole 2x2x4 slice. The times are simulated.
32 devices in a mesh: dp: 8 (over y, x, core), ctx: 4 (over z).
Axes of the slice: x: 2, y: 2, z: 4, core: 2. Of those that a mesh axis runs over, the one named last changes fastest.
Arguments:
- query: bfloat16 [4096, 4096], P(('dp', 'ctx')), may hold values from -6 to 6
- keys: bfloat16 [4096, 512], P(('dp', 'ctx')), may hold values from -6 to 6
- values: bfloat16 [4096, 512], P(('dp', 'ctx')), may hold values from -6 to 6
- cotangent: bfloat16 [4096, 4096], P(('dp', 'ctx')), may hold values from -6 to 6
- doc_lengths: int32 [64], replicated, may hold values from 1 to 128, 4096 in all
Outputs:
- key_grad: bfloat16 [4096, 512], P(('dp', 'ctx'))
- value_grad: bfloat16 [4096, 512], P(('dp', 'ctx'))
- query_bias_grad: float32 [4096], replicated
- value_bias_grad: float32 [512], replicated
Inputs may be any that keep to these rules, and one draw needn't show every extreme that they name: `doc_lengths`: 64 lengths that sum to 4096; the largest is exactly 128.
All inputs are finite; a program needn't handle non-finite values.
Results may differ from a plain program's by a relative error of at most 0.015.
Values may be sent and summed in bfloat16 or wider, within the bound.
No kernel may reach another device: no remote copies, remote signals or barrier semaphores. Data moves between devices by JAX's collectives and lax.ppermute only.
A program may use at most 64 MiB of HBM per device.

v0:
```python
import jax
import jax.numpy as jnp
from jax import lax
from jax.sharding import PartitionSpec as P

HEAD_DIM = 128
Q_HEADS = 32
KV_HEADS = 4


def from_behind(array, axis, by):
    size = lax.axis_size(axis)
    pairs = [(i, i + by) for i in range(size) if 0 <= i + by < size]
    return lax.ppermute(array, axis, pairs)


def segment_ids(ends, positions):
    return jnp.sum((ends[None, :] <= positions[:, None]).astype(jnp.int32), axis=1)


def attend(query_heads, grad_heads, query_pos, query_seg, key_rows, value_rows, key_pos, key_seg):
    tok_rows = query_heads.shape[0]
    groups = query_heads.shape[2]
    kv_feat = key_rows.shape[1]
    score_scale = HEAD_DIM ** (-0.5)
    num_steps = key_rows.shape[0] // tok_rows
    blocks = (
        key_rows.reshape(num_steps, tok_rows, KV_HEADS, HEAD_DIM),
        value_rows.reshape(num_steps, tok_rows, KV_HEADS, HEAD_DIM),
        key_pos.reshape(num_steps, tok_rows),
        key_seg.reshape(num_steps, tok_rows),
    )

    def allowed_of(block_pos, block_seg):
        return (query_seg[:, None] == block_seg[None, :]) & (
            block_pos[None, :] <= query_pos[:, None]
        )

    def scores_of(key_blk):
        return (
            jnp.einsum("qhgd,khd->hgqk", query_heads, key_blk, preferred_element_type=jnp.float32)
            * score_scale
        )

    def first_pass(state, block):
        key_blk, value_blk, block_pos, block_seg = block
        allowed = allowed_of(block_pos, block_seg)

        def first_update(inner):
            row_max, denominator, out_sum = inner
            scores = jnp.where(allowed, scores_of(key_blk), -1e30)
            new_max = jnp.maximum(row_max, jnp.max(scores, axis=-1))
            weights = jnp.where(allowed, jnp.exp(scores - new_max[..., None]), 0.0)
            factor = jnp.exp(row_max - new_max)
            denominator = denominator * factor + jnp.sum(weights, axis=-1)
            out_sum = out_sum * jnp.transpose(factor, (2, 0, 1))[..., None] + jnp.einsum(
                "hgqk,khd->qhgd",
                weights.astype(jnp.bfloat16),
                value_blk,
                preferred_element_type=jnp.float32,
            )
            return (new_max, denominator, out_sum)

        return (lax.cond(jnp.any(allowed), first_update, lambda inner: inner, state), None)

    start_state = (
        jnp.full((KV_HEADS, groups, tok_rows), -1e30, jnp.float32),
        jnp.zeros((KV_HEADS, groups, tok_rows), jnp.float32),
        jnp.zeros((tok_rows, KV_HEADS, groups, HEAD_DIM), jnp.float32),
    )
    (row_max, denominator, out_sum), _ = lax.scan(first_pass, start_state, blocks)
    log_total = row_max + jnp.log(denominator)
    output = out_sum / jnp.transpose(denominator, (2, 0, 1))[..., None]
    row_delta = jnp.transpose(jnp.sum(grad_heads.astype(jnp.float32) * output, axis=-1), (1, 2, 0))

    def second_pass(query_acc, block):
        key_blk, value_blk, block_pos, block_seg = block
        allowed = allowed_of(block_pos, block_seg)

        def second_update(accum):
            probs = jnp.where(allowed, jnp.exp(scores_of(key_blk) - log_total[..., None]), 0.0)
            probs_low = probs.astype(jnp.bfloat16)
            grad_probs = jnp.einsum(
                "qhgd,khd->hgqk", grad_heads, value_blk, preferred_element_type=jnp.float32
            )
            grad_scores = (probs * (grad_probs - row_delta[..., None])).astype(jnp.bfloat16)
            value_part = jnp.einsum(
                "hgqk,qhgd->khd", probs_low, grad_heads, preferred_element_type=jnp.float32
            )
            key_part = score_scale * jnp.einsum(
                "hgqk,qhgd->khd", grad_scores, query_heads, preferred_element_type=jnp.float32
            )
            column_sums = jnp.sum(grad_scores.astype(jnp.float32), axis=2)
            accum = accum + score_scale * jnp.einsum(
                "hgk,khd->hgd",
                column_sums,
                key_blk.astype(jnp.float32),
                precision=lax.Precision.HIGHEST,
            )
            return (accum, key_part, value_part)

        def passover(accum):
            empty = jnp.zeros((tok_rows, KV_HEADS, HEAD_DIM), jnp.float32)
            return (accum, empty, empty)

        query_acc, key_part, value_part = lax.cond(
            jnp.any(allowed), second_update, passover, query_acc
        )
        return (query_acc, (key_part, value_part))

    query_acc, (key_parts, value_parts) = lax.scan(
        second_pass, jnp.zeros((KV_HEADS, groups, HEAD_DIM), jnp.float32), blocks
    )
    return (key_parts.reshape(-1, kv_feat), value_parts.reshape(-1, kv_feat), query_acc.reshape(-1))


def body(query, keys, values, cotangent, doc_lengths):
    tok_rows = query.shape[0]
    kv_feat = keys.shape[1]
    groups = Q_HEADS // KV_HEADS
    reach = lax.axis_size("ctx") // 4
    device = lax.axis_index(("dp", "ctx"))
    ends = jnp.cumsum(doc_lengths)
    query_heads = query.reshape(tok_rows, KV_HEADS, groups, HEAD_DIM)
    grad_heads = cotangent.reshape(tok_rows, KV_HEADS, groups, HEAD_DIM)
    offsets = jnp.arange(tok_rows, dtype=jnp.int32)
    query_pos = device * tok_rows + offsets
    query_seg = segment_ids(ends, query_pos)
    key_list = [keys]
    value_list = [values]
    for distance in range(1, reach + 1):
        earlier_keys, earlier_values = from_behind((keys, values), ("dp", "ctx"), distance)
        key_list.append(earlier_keys)
        value_list.append(earlier_values)
    key_rows = jnp.concatenate(key_list, axis=0)
    value_rows = jnp.concatenate(value_list, axis=0)
    key_pos = jnp.concatenate(
        [(device - distance) * tok_rows + offsets for distance in range(reach + 1)]
    )
    key_seg = jnp.where(key_pos >= 0, segment_ids(ends, key_pos), -1)
    key_parts, value_parts, query_sum = attend(
        query_heads, grad_heads, query_pos, query_seg, key_rows, value_rows, key_pos, key_seg
    )
    terms = jnp.concatenate([key_parts, value_parts], axis=1)
    rounded = lax.optimization_barrier(terms.astype(jnp.bfloat16)).astype(jnp.float32)
    received = rounded[:tok_rows]
    for distance in range(1, reach + 1):
        outgoing = terms[distance * tok_rows : (distance + 1) * tok_rows].astype(jnp.bfloat16)
        returned = from_behind(outgoing, ("dp", "ctx"), -distance)
        received = received + returned.astype(jnp.float32)
    value_sums = jnp.sum(received[:, kv_feat:], axis=0)
    query_bias, value_bias = lax.psum((query_sum, value_sums), ("dp", "ctx"))
    key_grad = received[:, :kv_feat].astype(jnp.bfloat16)
    value_grad = received[:, kv_feat:].astype(jnp.bfloat16)
    return (key_grad, value_grad, query_bias, value_bias)


def solution(mesh):
    return jax.shard_map(
        body,
        mesh=mesh,
        in_specs=(
            P(("dp", "ctx"), None),
            P(("dp", "ctx"), None),
            P(("dp", "ctx"), None),
            P(("dp", "ctx"), None),
            P(),
        ),
        out_specs=(P(("dp", "ctx"), None), P(("dp", "ctx"), None), P(), P()),
        check_vma=False,
    )
```

profile of v0, /device:TPU:0, one launch (start us, length us, event | category | flops | bytes accessed | tf_op | source)
XLA Modules:
  0.0 106.9 jit_solution(5514990787544502868)
XLA Ops:
  0.6 5.6 %collective-permute-start.1 = (bf16[128,512]{1,0:T(8,128)(2,1)}, bf16[128,512]{1,0:T(8,128)(2,1)}, u32[]{:S(2)}, u32[]{:S(2)}) collective-permute-start(bf16[128,512]{1,0:T(8,128)(2,1)} %param.15), channel_id=1, source_target_pairs={{0,1},{1,2},{2,3},{3,4},{4,5},{5,6},{6,7},{7,8},{8,9},{9,10},{10,1... | collective-permute-start | bytes 393224 | tf_op jit(solution)/shard_map/ppermute | solution.py:14
  6.2 3.5 %collective-permute-start = (bf16[128,512]{1,0:T(8,128)(2,1)}, bf16[128,512]{1,0:T(8,128)(2,1)}, u32[]{:S(2)}, u32[]{:S(2)}) collective-permute-start(bf16[128,512]{1,0:T(8,128)(2,1)} %param.14), channel_id=1, source_target_pairs={{0,1},{1,2},{2,3},{3,4},{4,5},{5,6},{6,7},{7,8},{8,9},{9,10},{10,1... | collective-permute-start | bytes 393224 | tf_op jit(solution)/shard_map/ppermute | solution.py:14
  9.7 0.7 copy.34
  10.9 1.6 %copy.35 = bf16[128,4096]{0,1:T(8,128)(2,1)S(1)} copy(bf16[128,4096]{1,0:T(8,128)(2,1)} %param.13) | data formatting | bytes 2097152 | tf_op args[0]
  13.2 1.7 %copy.39 = bf16[128,4096]{0,1:T(8,128)(2,1)S(1)} copy(bf16[128,4096]{1,0:T(8,128)(2,1)} %param.16) | data formatting | bytes 2097152 | tf_op args[3]
  15.6 0.9 pad_maximum_fusion.1
  16.5 0.8 reshape.78
  17.3 1.0 copy.38
  18.3 1.7 %pad_maximum_fusion = bf16[256,512]{1,0:T(8,128)(2,1)} fusion(bf16[128,512]{1,0:T(8,128)(2,1)} %collective-permute-done, bf16[128,512]{1,0:T(8,128)(2,1)} %param.14), kind=kLoop, calls=%fused_computation.69 | loop fusion | flops 524288 | bytes 524288 | tf_op jit(solution)/shard_map/concatenate | solution.py:135
  19.9 1.7 %reshape.76 = bf16[2,128,4,128]{3,2,1,0:T(4,128)(2,1)} reshape(bf16[256,512]{1,0:T(8,128)(2,1)} %pad_maximum_fusion) | data formatting | bytes 524288 | tf_op jit(solution)/shard_map/reshape | solution.py:28
  21.6 1.7 %copy.41 = bf16[2,128,4,128]{3,1,2,0:T(8,128)(2,1)} copy(bf16[2,128,4,128]{3,2,1,0:T(4,128)(2,1)} %reshape.76) | data formatting | bytes 524288
  23.3 1.6 %broadcast_in_dim.74 = f32[128,4,8,128]{3,0,2,1:T(8,128)} broadcast(f32[]{:T(128)} %constant.91.clone.1), dimensions={} | broadcast | bytes 2097156 | tf_op jit(solution)/shard_map/broadcast_in_dim | solution.py:69
  24.9 7.4 %while.33 = (s32[]{:T(128)}, f32[4,8,128]{2,1,0:T(8,128)S(1)}, f32[4,8,128]{2,1,0:T(8,128)S(1)}, f32[128,4,8,128]{3,0,2,1:T(8,128)}, s32[128]{0:T(128)S(1)}, /*i...) while((s32[]{:T(128)}, f32[4,8,128]{2,1,0:T(8,128)S(1)}, ...), condition=%wide.region_9.10_spmd.clone, body=%wide.region_3.9_spmd.clone.sunk | while | flops 276377728 | bytes 28906808 | solution.py:71
  24.9 0.7 fusion.62
  26.3 4.5 %conditional.6 = ((f32[4,8,128]{2,1,0:T(8,128)S(1)}, f32[4,8,128]{2,1,0:T(8,128)S(1)}, f32[128,4,8,128]{3,0,2,1:T(8,128)})) conditional(s32[]{:T(128)} %convert_element_type.70, (f32[4,8,128]{2,1,0:T(8,128)S(1)}, f32[4,8,128]{2,1,0:T(8,128)S(1)}, f32[128,4,8,128]{3,0,2,1:T(8,128)}) %tuple.93, (pred[128,128]{0,1:T(8,128)(4,1)S(1)}, ...), branch_computations={%region_5.5_spmd, %region_6.8_spmd} | conditional | flops 276312064 | bytes 28885596 | solution.py:64
  26.4 1.5 %fusion.4 = (f32[4,8,128]{2,1,0:T(8,128)S(1)}, f32[4,128,128,8]{2,1,3,0:T(8,128)S(1)}) fusion(pred[128,128]{0,1:T(8,128)(4,1)S(1)} %get-tuple-element.234, bf16[128,4,8,128]{3,0,2,1:T(8,128)(2,1)S(1)} %get-tuple-element.237, bf16[2,128,4,128]{3,1,2,0:T(8,128)(2,1)} %get-tuple-element.235, s32[]{:T(128)} %get-tuple-element.236), kind=kOutput, calls=%fused_computation.5 | convolution fusion | flops 135786496 | bytes 3310080 | tf_op jit(solution)/shard_map/while/body/eval_jaxpr/cond/branch_1_fun/qhgd,khd->hgqk/dot_general | solution.py:41
  28.0 1.4 %bitcast_add_fusion = f32[128,4,8,128]{3,0,2,1:T(8,128)S(1)} fusion(f32[128,4,8,128]{3,0,2,1:T(8,128)S(1)} %copy-done, f32[4,128,128,8]{2,1,3,0:T(8,128)S(1)} %get-tuple-element.470, f32[128,4,8]{0,2,1:T(8,128)S(1)} %get-tuple-element.463, f32[4,8,128]{2,1,0:T(8,128)S(1)} %get-tuple-element.666, pred[128,128]{0,1:T(8,128)(4,1)S(1)} %get-tuple-element.234, ...), kind=kOutput, calls=%fused_computation.2 | convolution fusion | flops 137887744 | bytes 6471684 | tf_op jit(solution)/shard_map/while/body/eval_jaxpr/cond/branch_1_fun/hgqk,khd->qhgd/dot_general | solution.py:56
  30.0 0.8 copy-done.1
  30.9 0.7 fusion.62
  32.3 2.9 %copy.40 = f32[128,4,8,128]{0,3,2,1:T(8,128)} copy(f32[128,4,8,128]{3,0,2,1:T(8,128)} %get-tuple-element.295) | data formatting | bytes 4194304 | tf_op jit(solution)/shard_map/while | solution.py:71
  35.2 2.0 %multiply_reduce_fusion = f32[128,4,8]{0,2,1:T(8,128)S(1)} fusion(f32[128,4,8,128]{0,3,2,1:T(8,128)} %copy.40, f32[128,4,8]{0,2,1:T(8,128)S(1)} %bitcast.120, bf16[128,4096]{0,1:T(8,128)(2,1)S(1)} %copy.39), kind=kLoop, calls=%fused_computation.63 | loop fusion | flops 2093056 | bytes 3178496 | tf_op jit(solution)/shard_map/reduce_sum | solution.py:74
  37.2 9.9 %while.34 = (s32[]{:T(128)}, f32[4,8,128]{2,1,0:T(8,128)S(1)}, bf16[2,128,4,128]{3,2,1,0:T(4,128)(2,1)}, bf16[2,128,4,128]{3,2,1,0:T(4,128)(2,1)}, s32[128]{0:T(...) while((s32[]{:T(128)}, f32[4,8,128]{2,1,0:T(8,128)S(1)}, ...), condition=%wide.region_16.17_spmd.clone, body=%wide.region_11.16_spmd.clone.sunk | while | flops 548081792 | bytes 19142040 | solution.py:111
  37.3 0.7 fusion.65
  38.7 3.9 %conditional.7 = (f32[4,8,128]{2,1,0:T(8,128)S(1)}, bf16[1,128,4,128]{3,1,2,0:T(8,128)(2,1)S(1)}, bf16[1,128,4,128]{3,1,2,0:T(8,128)(2,1)S(1)}) conditional(s32[]{:T(128)} %convert_element_type.71, f32[4,8,128]{2,1,0:T(8,128)S(1)} %get-tuple-element.727, (pred[128,128]{1,0:T(8,128)(4,1)S(1)}, bf16[2,128,4,128]{3,1,2,0:T(8,128)(2,1)}, s32[]{:T(128)}, ...), branch_computations={%region_13.13_spmd, %region_14.15_spmd} | conditional | flops 548016128 | bytes 14402108 | solution.py:106
  38.7 1.7 %fusion.27 = f32[4,8,128,128]{3,2,1,0:T(8,128)S(1)} fusion(bf16[128,4,8,128]{3,0,2,1:T(8,128)(2,1)S(1)} %get-tuple-element.260, f32[4,8,128]{2,1,0:T(8,128)S(1)} %get-tuple-element.261, pred[128,128]{1,0:T(8,128)(4,1)S(1)} %get-tuple-element.257, bf16[2,128,4,128]{3,1,2,0:T(8,128)(2,1)} %get-tuple-element.258, s32[]{:T(128)} %get-tuple-element.259), kind=kOutput, calls=%fused_computation.31 | convolution fusion | flops 135790592 | bytes 3310080 | tf_op jit(solution)/shard_map/while/body/eval_jaxpr/cond/branch_1_fun/qhgd,khd->hgqk/dot_general | solution.py:41
  40.4 0.8 convert_reduce_fusion
  45.2 0.8 copy-done.3
  47.1 1.0 copy.68
  48.1 1.0 copy.69
  49.2 1.3 %collective-permute-start.2 = (bf16[128,1024]{1,0:T(8,128)(2,1)S(1)}, bf16[128,1024]{1,0:T(8,128)(2,1)S(1)}, u32[]{:S(2)}, u32[]{:S(2)}) collective-permute-start(bf16[128,1024]{1,0:T(8,128)(2,1)S(1)} %slice.24), channel_id=1, source_target_pairs={{1,0},{2,1},{3,2},{4,3},{5,4},{6,5},{7,6},{8,7},{9,8},{10,9},{11,1... | collective-permute-start | bytes 786440 | tf_op jit(solution)/shard_map/ppermute | solution.py:14
  50.5 7.0 %collective-permute-done.2 = bf16[128,1024]{1,0:T(8,128)(2,1)S(1)} collective-permute-done((bf16[128,1024]{1,0:T(8,128)(2,1)S(1)}, bf16[128,1024]{1,0:T(8,128)(2,1)S(1)}, u32[]{:S(2)}, u32[]{:S(2)}) %collective-permute-start.2) | collective-permute-done | bytes 262176 | tf_op jit(solution)/shard_map/ppermute | solution.py:14
  58.3 48.6 %all-reduce = (f32[4096]{0:T(1024)}, f32[512]{0:T(512)}) all-reduce(f32[4096]{0:T(1024)S(1)} %bitcast.123, f32[512]{0:T(512)S(1)} %slice_reduce_fusion), channel_id=1, replica_groups=mesh['dp'=8,'ctx'=4] {'dp','ctx'}, use_global_device_ids=true, to_apply=%region_17.18 | all-reduce | flops 4608 | bytes 36864 | tf_op jit(solution)/shard_map/psum | solution.py:152
  (68 shorter events, 7.7 us)
Async XLA Ops:
  0.6 14.9 %collective-permute-start.1 = (bf16[128,512]{1,0:T(8,128)(2,1)}, bf16[128,512]{1,0:T(8,128)(2,1)}, u32[]{:S(2)}, u32[]{:S(2)}) collective-permute-start(bf16[128,512]{1,0:T(8,128)(2,1)} %param.15), channel_id=1, source_target_pairs={{0,1},{1,2},{2,3},{3,4},{4,5},{5,6},{6,7},{7,8},{8,9},{9,10},{10,1... | collective-permute-start | bytes 393224 | tf_op jit(solution)/shard_map/ppermute | solution.py:14
  6.2 12.0 %collective-permute-start = (bf16[128,512]{1,0:T(8,128)(2,1)}, bf16[128,512]{1,0:T(8,128)(2,1)}, u32[]{:S(2)}, u32[]{:S(2)}) collective-permute-start(bf16[128,512]{1,0:T(8,128)(2,1)} %param.14), channel_id=1, source_target_pairs={{0,1},{1,2},{2,3},{3,4},{4,5},{5,6},{6,7},{7,8},{8,9},{9,10},{10,1... | collective-permute-start | bytes 393224 | tf_op jit(solution)/shard_map/ppermute | solution.py:14
  13.2 2.4 %copy-start.7 = (bf16[128,512]{1,0:T(8,128)(2,1)S(1)}, bf16[128,512]{1,0:T(8,128)(2,1)}, u32[]{:S(2)}) copy-start(bf16[128,512]{1,0:T(8,128)(2,1)} %param.15) | copy-start | bytes 393220
  26.3 1.7 %copy-start = (f32[128,4,8,128]{3,0,2,1:T(8,128)S(1)}, f32[128,4,8,128]{3,0,2,1:T(8,128)}, u32[]{:S(2)}) copy-start(f32[128,4,8,128]{3,0,2,1:T(8,128)} %get-tuple-element.239) | copy-start | bytes 6291460 | tf_op jit(solution)/shard_map/while/body/eval_jaxpr/cond
  29.4 1.4 %copy-start.1 = (f32[128,4,8,128]{3,0,2,1:T(8,128)}, f32[128,4,8,128]{3,0,2,1:T(8,128)S(1)}, u32[]{:S(2)}) copy-start(f32[128,4,8,128]{3,0,2,1:T(8,128)S(1)} %bitcast_add_fusion) | copy-start | bytes 6291460 | tf_op jit(solution)/shard_map/while/body/eval_jaxpr/cond
  38.7 4.0 %copy-start.3 = (bf16[2,128,4,128]{3,2,1,0:T(4,128)(2,1)S(1)}, bf16[2,128,4,128]{3,2,1,0:T(4,128)(2,1)}, u32[]{:S(2)}) copy-start(bf16[2,128,4,128]{3,2,1,0:T(4,128)(2,1)} %get-tuple-element.728) | copy-start | bytes 786436 | tf_op jit(solution)/shard_map/while
  38.7 4.0 %copy-start.5 = (bf16[2,128,4,128]{3,2,1,0:T(4,128)(2,1)S(1)}, bf16[2,128,4,128]{3,2,1,0:T(4,128)(2,1)}, u32[]{:S(2)}) copy-start(bf16[2,128,4,128]{3,2,1,0:T(4,128)(2,1)} %get-tuple-element.729) | copy-start | bytes 786436 | tf_op jit(solution)/shard_map/while
  40.4 1.0 copy-start.2
  42.9 0.7 copy-start.4
  42.9 0.8 copy-start.6
  45.1 1.0 copy-start.3
  45.1 1.0 copy-start.5
  46.3 0.7 copy-start.4
  46.4 0.8 copy-start.6
  49.2 8.3 %collective-permute-start.2 = (bf16[128,1024]{1,0:T(8,128)(2,1)S(1)}, bf16[128,1024]{1,0:T(8,128)(2,1)S(1)}, u32[]{:S(2)}, u32[]{:S(2)}) collective-permute-start(bf16[128,1024]{1,0:T(8,128)(2,1)S(1)} %slice.24), channel_id=1, source_target_pairs={{1,0},{2,1},{3,2},{4,3},{5,4},{6,5},{7,6},{8,7},{9,8},{10,9},{11,1... | collective-permute-start | bytes 786440 | tf_op jit(solution)/shard_map/ppermute | solution.py:14
where the time goes:
time: 108 us; the launch traced here: 107 us
  blocking collectives  48.6 us (45%)
  local copies, waits for them, and re-layouts  21.7 us (20%)
  starting transfers between devices  10.4 us (10%)
  other arithmetic  8.72 us (8%)
  waiting for transfers between devices  6.97 us (6%)
  matrix products  6.73 us (6%)
  loops' own time  3 us (3%)
    psum x1, blocking collectives, body(): query_bias, value_bias = lax.psum((query_sum, value_sums), ('dp', 'ctx'))  48.6 us
    ppermute x3, starting transfers between devices, from_behind(): return lax.ppermute(array, axis, pairs)  10.4 us
    unnamed x10, local copies, waits for them, and re-layouts  9.24 us
    ppermute x3, waiting for transfers between devices, from_behind(): return lax.ppermute(array, axis, pairs)  6.97 us
    dot_general x2, matrix products, scores_of(): jnp.einsum('qhgd,khd->hgqk', query_heads, key_blk, preferred_element_type...  3.24 us
    while x1, local copies, waits for them, and re-layouts, attend(): lax.scan(first_pass, start_state, blocks)  2.9 us
    while x16, local copies, waits for them, and re-layouts  2.49 us
  transfers between devices with their start and end apart: 3, of which 1 were waited for; matrix products, arithmetic and copies ran while one was open for 8% of the time, Pallas kernels for 0%

commit v1 on v0

v1 whole, which is shorter than its diff:
```python
import functools

import jax
import jax.numpy as jnp
from jax import lax
from jax.experimental import pallas as pl
from jax.experimental.pallas import tpu as pltpu
from jax.sharding import PartitionSpec as P

HEAD_DIM = 128
Q_HEADS = 32
KV_HEADS = 4
GROUP = Q_HEADS // KV_HEADS
AXES = ("dp", "ctx")
SCALE = HEAD_DIM ** (-0.5)
LOG2E = 1.4426950408889634
NT = (((1,), (1,)), ((), ()))
TN = (((0,), (0,)), ((), ()))
NN = (((1,), (0,)), ((), ()))


def dot(a, b, dims):
    return lax.dot_general(a, b, dims, preferred_element_type=jnp.float32)


def attend_kernel(reach, start_ref, q_ref, c_ref, k_ref, v_ref, *refs):
    kp_refs, vp_refs = refs[:reach], refs[reach : 2 * reach]
    own_ref, *back_refs = refs[2 * reach : 3 * reach + 1]
    bias_ref, p_ref, g_ref = refs[3 * reach + 1 :]
    rows = q_ref.shape[0]
    wide = 2 * rows
    kv_feat = k_ref.shape[1]
    key_row = lax.broadcasted_iota(jnp.int32, (rows, wide), 0)
    query_col = lax.broadcasted_iota(jnp.int32, (rows, wide), 1) & (rows - 1)
    start = start_ref[...]
    start = jnp.concatenate([start, start], axis=1)
    near = key_row <= query_col
    folded = jnp.where(near, key_row, key_row - reach * rows)
    valids = [folded >= start] + [key_row - j * rows >= start for j in range(1, reach)]
    lane = lax.broadcasted_iota(jnp.int32, (rows, HEAD_DIM), 1)
    order = [reach] + list(range(1, reach))
    for g in range(KV_HEADS):
        cols = slice(g * HEAD_DIM, (g + 1) * HEAD_DIM)
        key_all = jnp.concatenate([k_ref[:, cols]] + [kp_refs[j - 1][:, cols] for j in order], axis=0)
        value_all = jnp.concatenate([v_ref[:, cols]] + [vp_refs[j - 1][:, cols] for j in order], axis=0)
        q_list, c_list = [], []
        for pair in range(GROUP // 2):
            heads = [g * GROUP + 2 * pair + i for i in range(2)]
            q_two = [q_ref[:, h * HEAD_DIM : (h + 1) * HEAD_DIM] for h in heads]
            c_two = [c_ref[:, h * HEAD_DIM : (h + 1) * HEAD_DIM] for h in heads]
            for i in range(2):
                indicator = jnp.where(lane == 2 * pair + i, 1.0, 0.0).astype(jnp.bfloat16)
                q_list.append(jnp.concatenate([q_two[i], indicator], axis=1))
            c_list += c_two
            s_all = dot(key_all, jnp.concatenate(q_two, axis=0), NT)
            d_all = dot(value_all, jnp.concatenate(c_two, axis=0), NT)

            def parts(whole):
                cut = [whole[i * rows : (i + 1) * rows] for i in range(reach + 1)]
                return [jnp.where(near, cut[0], cut[1])] + cut[2:]

            s_parts = [jnp.where(ok, s * (SCALE * LOG2E), -1e30) for ok, s in zip(valids, parts(s_all))]
            d_parts = parts(d_all)
            top = functools.reduce(jnp.maximum, [jnp.max(s, axis=0, keepdims=True) for s in s_parts])
            e_parts = [jnp.exp2(s - top) for s in s_parts]
            total = sum(jnp.sum(e, axis=0, keepdims=True) for e in e_parts)
            inv = 1.0 / total
            delta = inv * sum(jnp.sum(e * d, axis=0, keepdims=True) for e, d in zip(e_parts, d_parts))
            at = slice(pair * wide, (pair + 1) * wide)
            for i, (e, d) in enumerate(zip(e_parts, d_parts)):
                prob = e * inv
                grad = prob * (d - delta)
                if i == 0:
                    p_ref[:rows, at] = jnp.where(near, prob, 0.0).astype(jnp.bfloat16)
                    g_ref[:rows, at] = jnp.where(near, grad, 0.0).astype(jnp.bfloat16)
                    p_ref[rows : 2 * rows, at] = jnp.where(near, 0.0, prob).astype(jnp.bfloat16)
                    g_ref[rows : 2 * rows, at] = jnp.where(near, 0.0, grad).astype(jnp.bfloat16)
                else:
                    p_ref[(i + 1) * rows : (i + 2) * rows, at] = prob.astype(jnp.bfloat16)
                    g_ref[(i + 1) * rows : (i + 2) * rows, at] = grad.astype(jnp.bfloat16)
        value_part = dot(p_ref[...], jnp.concatenate(c_list, axis=0), NN)
        key_wide = dot(g_ref[...], jnp.concatenate(q_list, axis=0), NN)
        key_part = (key_wide[:, :HEAD_DIM] * SCALE).astype(jnp.bfloat16)
        value_part = value_part.astype(jnp.bfloat16)
        for i, ref in enumerate([own_ref] + [back_refs[j - 1] for j in order]):
            ref[:, g * HEAD_DIM : (g + 1) * HEAD_DIM] = key_part[i * rows : (i + 1) * rows]
            ref[:, kv_feat + g * HEAD_DIM : kv_feat + (g + 1) * HEAD_DIM] = value_part[i * rows : (i + 1) * rows]
        bias_ref[Q_HEADS + g : Q_HEADS + g + 1, :] = jnp.sum(value_part.astype(jnp.float32), axis=0, keepdims=True)
        sums = key_wide[:, HEAD_DIM:] * SCALE
        high = sums.astype(jnp.bfloat16)
        low = (sums - high.astype(jnp.float32)).astype(jnp.bfloat16)
        query_bias = dot(high, key_all, TN) + dot(low, key_all, TN)
        bias_ref[g * GROUP : (g + 1) * GROUP, :] = query_bias[:GROUP]


def attend(reach, start, query, cotangent, keys, values, far_keys, far_values):
    rows = query.shape[0]
    kv_feat = keys.shape[1]
    window = (reach + 1) * rows
    block = jax.ShapeDtypeStruct((rows, 2 * kv_feat), jnp.bfloat16)
    vmem = pl.BlockSpec(memory_space=pltpu.VMEM)
    return pl.pallas_call(
        functools.partial(attend_kernel, reach),
        out_shape=[block] * (reach + 1) + [jax.ShapeDtypeStruct((Q_HEADS + KV_HEADS, HEAD_DIM), jnp.float32)],
        in_specs=[vmem] * (5 + 2 * reach),
        out_specs=[vmem] * (reach + 2),
        scratch_shapes=[
            pltpu.VMEM((window, GROUP * rows), jnp.bfloat16),
            pltpu.VMEM((window, GROUP * rows), jnp.bfloat16),
        ],
        compiler_params=pltpu.CompilerParams(vmem_limit_bytes=32 * 1024 * 1024),
        cost_estimate=pl.CostEstimate(flops=2 * 4 * window * rows * Q_HEADS * HEAD_DIM, bytes_accessed=3 << 20, transcendentals=window * rows * Q_HEADS),
    )(start, query, cotangent, keys, values, *far_keys, *far_values)


def shift(array, count, by):
    return lax.ppermute(array, AXES, [(i, (i + by) % count) for i in range(count)])


def all_sum(array, count):
    step = 1
    steps = []
    while step < count:
        steps.append(step)
        step *= 2
    for step in steps:
        array = array + lax.ppermute(array, AXES, [(i, i ^ step) for i in range(count)])
    return array


def body(query, keys, values, cotangent, doc_lengths):
    rows = query.shape[0]
    kv_feat = keys.shape[1]
    count = lax.axis_size("dp") * lax.axis_size("ctx")
    reach = lax.axis_size("ctx") // 4
    device = lax.axis_index(AXES)
    far_keys = [shift(keys, count, distance) for distance in range(1, reach + 1)]
    far_values = [shift(values, count, distance) for distance in range(1, reach + 1)]
    ends = jnp.cumsum(doc_lengths)
    position = device * rows + jnp.arange(rows, dtype=jnp.int32)
    start = jnp.max(jnp.where(ends[:, None] <= position[None, :], ends[:, None], 0), axis=0)
    start = (start - device * rows)[None, :]
    own, *rest = attend(reach, start, query, cotangent, keys, values, far_keys, far_values)
    *backs, bias = rest
    bias = all_sum(bias, count)
    received = own.astype(jnp.float32)
    for distance in range(1, reach + 1):
        received = received + shift(backs[distance - 1], count, -distance).astype(jnp.float32)
    received = received.astype(jnp.bfloat16)
    query_bias = bias[:Q_HEADS].reshape(-1)
    value_bias = bias[Q_HEADS:].reshape(-1)
    return (received[:, :kv_feat], received[:, kv_feat:], query_bias, value_bias)


def solution(mesh):
    return jax.shard_map(
        body,
        mesh=mesh,
        in_specs=(P(AXES, None),) * 4 + (P(),),
        out_specs=(P(AXES, None), P(AXES, None), P(), P()),
        check_vma=False,
    )
```

time: 108 us -> 44.7 us (0.41)
  blocking collectives: 48.6 us -> 0 us
  waiting for transfers between devices: 6.97 us -> 24.9 us
  local copies, waits for them, and re-layouts: 21.7 us -> 6.01 us
  other arithmetic: 8.72 us -> 0.4 us
  matrix products: 6.73 us -> 0 us
  Pallas kernels: 0 us -> 4.37 us
  loops' own time: 3 us -> 0 us
  starting transfers between devices: 10.4 us -> 8.16 us
    psum x1 -> x0, blocking collectives: 48.6 us -> none  [body(): query_bias, value_bias = lax.psum((query_sum, value_sums), ('dp', 'ctx'))]
    ppermute x3 -> x8, waiting for transfers between devices: 6.97 us -> 24.9 us  [the longest x5 13.9 us: all_sum(): lax.ppermute(array, AXES, [(i, i ^ step) for i in range(count)])]
    dot_general x7 -> x0, matrix products: 6.73 us -> none  [the longest x2 3.24 us: scores_of(): jnp.einsum('qhgd,khd->hgqk', query_heads, key_blk, preferred_element_type...]
    unnamed x10 -> x8, local copies, waits for them, and re-layouts: 9.24 us -> 3.36 us
    while x17 -> x0, local copies, waits for them, and re-layouts: 5.39 us -> none  [the longest x1 2.9 us: attend(): lax.scan(first_pass, start_state, blocks)]
    pallas_call x0 -> x1, Pallas kernels: none -> 4.37 us  [attend(): pl.pallas_call(functools.partial(attend_kernel, reach), out_shape=[block]...]
    another operation x6 -> x0, loops' own time: 3 us -> none  [the longest x1 1.46 us: attend(): lax.scan(second_pass, jnp.zeros((KV_HEADS, groups, HEAD_DIM), jnp.float32...]
    reduce_or x4 -> x0, other arithmetic: 2.94 us -> none  [the longest x2 1.47 us: first_pass(): jnp.any(allowed)]
  transfers between devices with their start and end apart: 3 -> 8, of which waited for: 1 -> 8; matrix products, arithmetic and copies ran while one was open for 8% -> 5% of each run, Pallas kernels for 0% -> 0%
where the time goes in v1:
time: 44.7 us; the launch traced here: 44.5 us
  waiting for transfers between devices  24.9 us (56%)
  starting transfers between devices  8.16 us (18%)
  local copies, waits for them, and re-layouts  6.01 us (13%)
  Pallas kernels  4.37 us (10%)
  between operations  0.69 us (2%)
    ppermute x5, waiting for transfers between devices, all_sum(): lax.ppermute(array, AXES, [(i, i ^ step) for i in range(count)])  13.9 us
    ppermute x3, waiting for transfers between devices, shift(): lax.ppermute(array, AXES, [(i, (i + by) % count) for i in range(count)])  11 us
    ppermute x3, starting transfers between devices, shift(): lax.ppermute(array, AXES, [(i, (i + by) % count) for i in range(count)])  4.66 us
    pallas_call x1, Pallas kernels, attend(): pl.pallas_call(functools.partial(attend_kernel, reach), out_shape=[block]...  4.37 us
    ppermute x5, starting transfers between devices, all_sum(): lax.ppermute(array, AXES, [(i, i ^ step) for i in range(count)])  3.5 us
    unnamed x8, local copies, waits for them, and re-layouts  3.36 us
  transfers between devices with their start and end apart: 8, of which 8 were waited for; matrix products, arithmetic and copies ran while one was open for 5% of the time, Pallas kernels for 0%

profile of v1, /device:TPU:0, one launch (start us, length us, event | category | flops | bytes accessed | tf_op | source)
XLA Modules:
  0.0 44.5 jit_solution(13363230150001307086)
XLA Ops:
  0.6 0.0 copy-start.2
  0.6 3.1 %collective-permute-start = (bf16[128,512]{1,0:T(8,128)(2,1)}, bf16[128,512]{1,0:T(8,128)(2,1)S(1)}, u32[]{:S(2)}, u32[]{:S(2)}) collective-permute-start(bf16[128,512]{1,0:T(8,128)(2,1)} %k_ref.1), channel_id=1, source_target_pairs={{0,1},{1,2},{2,3},{3,4},{4,5},{5,6},{6,7},{7,8},{8,9},{9,10},{10,1... | collective-permute-start | bytes 393224 | tf_op jit(solution)/shard_map/ppermute | solution.py:117
  3.7 1.6 %collective-permute-start.1 = (bf16[128,512]{1,0:T(8,128)(2,1)}, bf16[128,512]{1,0:T(8,128)(2,1)S(1)}, u32[]{:S(2)}, u32[]{:S(2)}) collective-permute-start(bf16[128,512]{1,0:T(8,128)(2,1)} %v_ref.1), channel_id=1, source_target_pairs={{0,1},{1,2},{2,3},{3,4},{4,5},{5,6},{6,7},{7,8},{8,9},{9,10},{10,1... | collective-permute-start | bytes 393224 | tf_op jit(solution)/shard_map/ppermute | solution.py:117
  5.3 0.7 %copy.11 = s32[64,1]{1,0:T(8,128)S(1)} copy(s32[64,1]{0,1:T(1,128)} %bitcast.7) | data formatting | bytes 512 | tf_op jit(solution)/shard_map/reshape.32
  6.0 0.1 reduce-window.8
  6.1 0.1 reduce
  6.3 0.1 select_reduce_fusion
  6.4 4.1 %collective-permute-done.refs_0_ = bf16[128,512]{1,0:T(8,128)(2,1)S(1)} collective-permute-done((bf16[128,512]{1,0:T(8,128)(2,1)}, bf16[128,512]{1,0:T(8,128)(2,1)S(1)}, u32[]{:S(2)}, u32[]{:S(2)}) %collective-permute-start) | collective-permute-done | bytes 131104 | tf_op jit(solution)/shard_map/ppermute | solution.py:117
  10.5 2.8 %collective-permute-done.1.refs_1_ = bf16[128,512]{1,0:T(8,128)(2,1)S(1)} collective-permute-done((bf16[128,512]{1,0:T(8,128)(2,1)}, bf16[128,512]{1,0:T(8,128)(2,1)S(1)}, u32[]{:S(2)}, u32[]{:S(2)}) %collective-permute-start.1) | collective-permute-done | bytes 131104 | tf_op jit(solution)/shard_map/ppermute | solution.py:117
  13.3 0.0 copy-done.2
  13.3 0.0 copy-start
  13.3 1.2 %copy-done = bf16[128,4096]{1,0:T(8,128)(2,1)S(1)} copy-done((bf16[128,4096]{1,0:T(8,128)(2,1)S(1)}, bf16[128,4096]{1,0:T(8,128)(2,1)}, u32[]{:S(2)}) %copy-start) | copy-done | bytes 1048600
  14.6 0.0 copy-start.1
  14.6 1.2 %copy-done.1 = bf16[128,4096]{1,0:T(8,128)(2,1)S(1)} copy-done((bf16[128,4096]{1,0:T(8,128)(2,1)S(1)}, bf16[128,4096]{1,0:T(8,128)(2,1)}, u32[]{:S(2)}) %copy-start.1) | copy-done | bytes 1048600
  15.8 0.9 %copy-done.3 = bf16[128,512]{1,0:T(8,128)(2,1)S(1)} copy-done((bf16[128,512]{1,0:T(8,128)(2,1)S(1)}, bf16[128,512]{1,0:T(8,128)(2,1)}, u32[]{:S(2)}) %copy-start.3) | copy-done | bytes 131096
  16.7 4.4 %shard_map.84 = (bf16[128,1024]{1,0:T(8,128)(2,1)S(1)}, bf16[128,1024]{1,0:T(8,128)(2,1)S(1)}, f32[36,128]{1,0:T(8,128)S(1)}) custom-call(s32[1,128]{1,0:T(1,128)S(1)} %subtract_bitcast_fusion.start_ref, bf16[128,4096]{1,0:T(8,128)(2,1)S(1)} %copy-done, bf16[128,4096]{1,0:T(8,128)(2,1)S(1)} %copy-done.1, bf16[128,512]{1,0:T(8,128)(2,1)S(1)} %copy-done.2, ...), custom_call_target="tpu_custom_call" | custom-call | flops 1073741824 | bytes 3145728 | tf_op jit(solution)/shard_map/pallas_call | solution.py:102
  21.1 0.1 collective-permute-start.3
  21.1 3.8 %collective-permute-done.3 = f32[36,128]{1,0:T(8,128)S(1)} collective-permute-done((f32[36,128]{1,0:T(8,128)S(1)}, f32[36,128]{1,0:T(8,128)S(1)}, u32[]{:S(2)}, u32[]{:S(2)}) %collective-permute-start.3) | collective-permute-done | bytes 18464 | tf_op jit(solution)/shard_map/ppermute | solution.py:127
  24.9 0.0 collective-permute-start.4
  24.9 4.7 %collective-permute-done.4 = f32[36,128]{1,0:T(8,128)S(1)} collective-permute-done((f32[36,128]{1,0:T(8,128)S(1)}, f32[36,128]{1,0:T(8,128)S(1)}, u32[]{:S(2)}, u32[]{:S(2)}) %collective-permute-start.4) | collective-permute-done | bytes 18464 | tf_op jit(solution)/shard_map/ppermute | solution.py:127
  29.6 0.0 collective-permute-start.5
  29.6 1.2 %collective-permute-done.5 = f32[36,128]{1,0:T(8,128)S(1)} collective-permute-done((f32[36,128]{1,0:T(8,128)S(1)}, f32[36,128]{1,0:T(8,128)S(1)}, u32[]{:S(2)}, u32[]{:S(2)}) %collective-permute-start.5) | collective-permute-done | bytes 18464 | tf_op jit(solution)/shard_map/ppermute | solution.py:127
  30.8 1.2 %collective-permute-start.6 = (f32[36,128]{1,0:T(8,128)S(1)}, f32[36,128]{1,0:T(8,128)S(1)}, u32[]{:S(2)}, u32[]{:S(2)}) collective-permute-start(f32[36,128]{1,0:T(8,128)S(1)} %add.37), channel_id=1, source_target_pairs={{0,8},{1,9},{2,10},{3,11},{4,12},{5,13},{6,14},{7,15},{8,0},{9,1},... | collective-permute-start | bytes 55304 | tf_op jit(solution)/shard_map/ppermute | solution.py:127
  32.1 2.5 %collective-permute-done.6 = f32[36,128]{1,0:T(8,128)S(1)} collective-permute-done((f32[36,128]{1,0:T(8,128)S(1)}, f32[36,128]{1,0:T(8,128)S(1)}, u32[]{:S(2)}, u32[]{:S(2)}) %collective-permute-start.6) | collective-permute-done | bytes 18464 | tf_op jit(solution)/shard_map/ppermute | solution.py:127
  34.6 2.2 %collective-permute-start.7 = (f32[36,128]{1,0:T(8,128)S(1)}, f32[36,128]{1,0:T(8,128)S(1)}, u32[]{:S(2)}, u32[]{:S(2)}) collective-permute-start(f32[36,128]{1,0:T(8,128)S(1)} %add.38), channel_id=1, source_target_pairs={{0,16},{1,17},{2,18},{3,19},{4,20},{5,21},{6,22},{7,23},{8,24},{9,... | collective-permute-start | bytes 55304 | tf_op jit(solution)/shard_map/ppermute | solution.py:127
  36.8 0.0 collective-permute-start.2
  36.8 1.8 %collective-permute-done.7 = f32[36,128]{1,0:T(8,128)S(1)} collective-permute-done((f32[36,128]{1,0:T(8,128)S(1)}, f32[36,128]{1,0:T(8,128)S(1)}, u32[]{:S(2)}, u32[]{:S(2)}) %collective-permute-start.7) | collective-permute-done | bytes 18464 | tf_op jit(solution)/shard_map/ppermute | solution.py:127
  38.5 0.6 %slice_bitcast_fusion.1 = f32[512]{0:T(512)} fusion(f32[36,128]{1,0:T(8,128)S(1)} %add.39), kind=kLoop, calls=%fused_computation.3 | loop fusion | bytes 4096 | tf_op jit(solution)/shard_map/reshape | solution.py:151
  39.1 0.6 %slice_bitcast_fusion = f32[4096]{0:T(1024)} fusion(f32[36,128]{1,0:T(8,128)S(1)} %add.39), kind=kLoop, calls=%fused_computation.2 | loop fusion | bytes 32768 | tf_op jit(solution)/shard_map/reshape | solution.py:150
  39.7 4.0 %collective-permute-done.2 = bf16[128,1024]{1,0:T(8,128)(2,1)S(1)} collective-permute-done((bf16[128,1024]{1,0:T(8,128)(2,1)S(1)}, bf16[128,1024]{1,0:T(8,128)(2,1)S(1)}, u32[]{:S(2)}, u32[]{:S(2)}) %collective-permute-start.2) | collective-permute-done | bytes 262176 | tf_op jit(solution)/shard_map/ppermute | solution.py:117
  43.7 0.1 add_convert_fusion
  43.8 0.7 %fusion = (bf16[128,512]{1,0:T(8,128)(2,1)}, bf16[128,512]{1,0:T(8,128)(2,1)}) fusion(bf16[128,1024]{1,0:T(8,128)(2,1)S(1)} %add_convert_fusion), kind=kLoop, calls=%fused_computation.6 | loop fusion | bytes 524288 | tf_op jit(solution)/shard_map/slice | solution.py:152
  (8 shorter events, 0.0 us)
Async XLA Ops:
  0.6 12.7 %copy-start.2 = (bf16[128,512]{1,0:T(8,128)(2,1)S(1)}, bf16[128,512]{1,0:T(8,128)(2,1)}, u32[]{:S(2)}) copy-start(bf16[128,512]{1,0:T(8,128)(2,1)} %k_ref.1) | copy-start | bytes 393220
  0.6 9.9 %collective-permute-start = (bf16[128,512]{1,0:T(8,128)(2,1)}, bf16[128,512]{1,0:T(8,128)(2,1)S(1)}, u32[]{:S(2)}, u32[]{:S(2)}) collective-permute-start(bf16[128,512]{1,0:T(8,128)(2,1)} %k_ref.1), channel_id=1, source_target_pairs={{0,1},{1,2},{2,3},{3,4},{4,5},{5,6},{6,7},{7,8},{8,9},{9,10},{10,1... | collective-permute-start | bytes 393224 | tf_op jit(solution)/shard_map/ppermute | solution.py:117
  3.7 9.6 %collective-permute-start.1 = (bf16[128,512]{1,0:T(8,128)(2,1)}, bf16[128,512]{1,0:T(8,128)(2,1)S(1)}, u32[]{:S(2)}, u32[]{:S(2)}) collective-permute-start(bf16[128,512]{1,0:T(8,128)(2,1)} %v_ref.1), channel_id=1, source_target_pairs={{0,1},{1,2},{2,3},{3,4},{4,5},{5,6},{6,7},{7,8},{8,9},{9,10},{10,1... | collective-permute-start | bytes 393224 | tf_op jit(solution)/shard_map/ppermute | solution.py:117
  13.3 1.2 %copy-start = (bf16[128,4096]{1,0:T(8,128)(2,1)S(1)}, bf16[128,4096]{1,0:T(8,128)(2,1)}, u32[]{:S(2)}) copy-start(bf16[128,4096]{1,0:T(8,128)(2,1)} %q_ref.1) | copy-start | bytes 3145732
  14.6 1.2 %copy-start.1 = (bf16[128,4096]{1,0:T(8,128)(2,1)S(1)}, bf16[128,4096]{1,0:T(8,128)(2,1)}, u32[]{:S(2)}) copy-start(bf16[128,4096]{1,0:T(8,128)(2,1)} %c_ref.1) | copy-start | bytes 3145732
  15.8 0.9 %copy-start.3 = (bf16[128,512]{1,0:T(8,128)(2,1)S(1)}, bf16[128,512]{1,0:T(8,128)(2,1)}, u32[]{:S(2)}) copy-start(bf16[128,512]{1,0:T(8,128)(2,1)} %v_ref.1) | copy-start | bytes 393220
  21.1 3.8 %collective-permute-start.3 = (f32[36,128]{1,0:T(8,128)S(1)}, f32[36,128]{1,0:T(8,128)S(1)}, u32[]{:S(2)}, u32[]{:S(2)}) collective-permute-start(f32[36,128]{1,0:T(8,128)S(1)} %get-tuple-element.9), channel_id=1, source_target_pairs={{0,1},{1,0},{2,3},{3,2},{4,5},{5,4},{6,7},{7,6},{8,9},{9,8},{10,11... | collective-permute-start | bytes 55304 | tf_op jit(solution)/shard_map/ppermute | solution.py:127
  24.9 4.7 %collective-permute-start.4 = (f32[36,128]{1,0:T(8,128)S(1)}, f32[36,128]{1,0:T(8,128)S(1)}, u32[]{:S(2)}, u32[]{:S(2)}) collective-permute-start(f32[36,128]{1,0:T(8,128)S(1)} %add.35), channel_id=1, source_target_pairs={{0,2},{1,3},{2,0},{3,1},{4,6},{5,7},{6,4},{7,5},{8,10},{9,11},{10,... | collective-permute-start | bytes 55304 | tf_op jit(solution)/shard_map/ppermute | solution.py:127
  29.6 1.2 %collective-permute-start.5 = (f32[36,128]{1,0:T(8,128)S(1)}, f32[36,128]{1,0:T(8,128)S(1)}, u32[]{:S(2)}, u32[]{:S(2)}) collective-permute-start(f32[36,128]{1,0:T(8,128)S(1)} %add.36), channel_id=1, source_target_pairs={{0,4},{1,5},{2,6},{3,7},{4,0},{5,1},{6,2},{7,3},{8,12},{9,13},{10,... | collective-permute-start | bytes 55304 | tf_op jit(solution)/shard_map/ppermute | solution.py:127
  30.8 3.8 %collective-permute-start.6 = (f32[36,128]{1,0:T(8,128)S(1)}, f32[36,128]{1,0:T(8,128)S(1)}, u32[]{:S(2)}, u32[]{:S(2)}) collective-permute-start(f32[36,128]{1,0:T(8,128)S(1)} %add.37), channel_id=1, source_target_pairs={{0,8},{1,9},{2,10},{3,11},{4,12},{5,13},{6,14},{7,15},{8,0},{9,1},... | collective-permute-start | bytes 55304 | tf_op jit(solution)/shard_map/ppermute | solution.py:127
  34.6 3.9 %collective-permute-start.7 = (f32[36,128]{1,0:T(8,128)S(1)}, f32[36,128]{1,0:T(8,128)S(1)}, u32[]{:S(2)}, u32[]{:S(2)}) collective-permute-start(f32[36,128]{1,0:T(8,128)S(1)} %add.38), channel_id=1, source_target_pairs={{0,16},{1,17},{2,18},{3,19},{4,20},{5,21},{6,22},{7,23},{8,24},{9,... | collective-permute-start | bytes 55304 | tf_op jit(solution)/shard_map/ppermute | solution.py:127
  36.8 6.9 %collective-permute-start.2 = (bf16[128,1024]{1,0:T(8,128)(2,1)S(1)}, bf16[128,1024]{1,0:T(8,128)(2,1)S(1)}, u32[]{:S(2)}, u32[]{:S(2)}) collective-permute-start(bf16[128,1024]{1,0:T(8,128)(2,1)S(1)} %get-tuple-element.8), channel_id=1, source_target_pairs={{0,31},{1,0},{2,1},{3,2},{4,3},{5,4},{6,5},{7,6},{8,7},{9,8},{10,9... | collective-permute-start | bytes 786440 | tf_op jit(solution)/shard_map/ppermute | solution.py:117

commit v2 on v1

v2 whole, which is shorter than its diff:
```python
import functools

import jax
import jax.numpy as jnp
from jax import lax
from jax.experimental import pallas as pl
from jax.experimental.pallas import tpu as pltpu
from jax.sharding import PartitionSpec as P

HEAD_DIM = 128
Q_HEADS = 32
KV_HEADS = 4
GROUP = Q_HEADS // KV_HEADS
AXES = ("dp", "ctx")
SCALE = HEAD_DIM ** (-0.5)
LOG2E = 1.4426950408889634
NT = (((1,), (1,)), ((), ()))
TN = (((0,), (0,)), ((), ()))
NN = (((1,), (0,)), ((), ()))


def dot(a, b, dims):
    return lax.dot_general(a, b, dims, preferred_element_type=jnp.float32)


def head(ref, h):
    return ref[:, h * HEAD_DIM : (h + 1) * HEAD_DIM]


def spill_of(start):
    return jnp.sum(jnp.where(start < 0, 1, 0), axis=1, keepdims=True)


def grids(rows, wide):
    key_row = lax.broadcasted_iota(jnp.int32, (rows, wide), 0)
    query_col = lax.broadcasted_iota(jnp.int32, (rows, wide), 1) & (rows - 1)
    return key_row, key_row <= query_col


def near_kernel(start_ref, q_ref, c_ref, k_ref, v_ref, s_ref, d_ref, sum_ref):
    rows = q_ref.shape[0]
    key_row, near = grids(rows, 2 * rows)
    start = jnp.concatenate([start_ref[...]] * 2, axis=1)
    valid = near & (key_row >= start)
    for pair in range(Q_HEADS // 2):
        kv = 2 * pair // GROUP
        at = slice(2 * pair * rows, 2 * (pair + 1) * rows)
        q_two = jnp.concatenate([head(q_ref, 2 * pair), head(q_ref, 2 * pair + 1)], axis=0)
        c_two = jnp.concatenate([head(c_ref, 2 * pair), head(c_ref, 2 * pair + 1)], axis=0)
        s_ref[:, at] = jnp.where(valid, dot(head(k_ref, kv), q_two, NT) * (SCALE * LOG2E), -1e30)
        d_ref[:, at] = dot(head(v_ref, kv), c_two, NT)
    for g in range(KV_HEADS):
        heads = range(g * GROUP, (g + 1) * GROUP)
        total = sum(head(c_ref, h).astype(jnp.float32) for h in heads)
        sum_ref[g : g + 1, :] = jnp.sum(total, axis=0, keepdims=True)


def far_kernel(reach, start_ref, k_ref, q_ref, c_ref, s_ref, d_ref, sum_ref, *refs):
    kp_refs, vp_refs = refs[:reach], refs[reach : 2 * reach]
    bias_ref, p_ref, g_ref = refs[2 * reach :]
    rows = q_ref.shape[0]
    wide = 2 * rows
    key_row, near = grids(rows, wide)
    start = jnp.concatenate([start_ref[...]] * 2, axis=1)
    far = jnp.logical_not(near) & (key_row - reach * rows >= start)
    valids = [key_row - j * rows >= start for j in range(1, reach)]
    order = [reach] + list(range(1, reach))
    spill = spill_of(start_ref[...])
    lane = lax.broadcasted_iota(jnp.int32, (rows, HEAD_DIM), 1)
    row = lax.broadcasted_iota(jnp.int32, (rows, HEAD_DIM), 0)
    spilled = row < spill
    indicator = jnp.concatenate(
        [jnp.where(lane == jnp.where(spilled, i, i + GROUP), 1.0, 0.0).astype(jnp.bfloat16) for i in range(GROUP)], axis=0)
    far_sum = jnp.logical_not(spilled) & (lane < GROUP)
    bias_ref[Q_HEADS:, :] = sum_ref[:KV_HEADS]
    for g in range(KV_HEADS):
        far_key = jnp.concatenate([head(kp_refs[j - 1], g) for j in order], axis=0)
        far_value = jnp.concatenate([head(vp_refs[j - 1], g) for j in order], axis=0)
        for pair in range(GROUP // 2):
            first = g * GROUP + 2 * pair
            at = slice(first * rows, (first + 2) * rows)
            q_two = jnp.concatenate([head(q_ref, first), head(q_ref, first + 1)], axis=0)
            c_two = jnp.concatenate([head(c_ref, first), head(c_ref, first + 1)], axis=0)
            s_far = dot(far_key, q_two, NT)
            d_far = dot(far_value, c_two, NT)
            cut = [slice(i * rows, (i + 1) * rows) for i in range(reach)]
            s_parts = [jnp.where(far, s_far[cut[0]] * (SCALE * LOG2E), s_ref[:, at])]
            s_parts += [jnp.where(ok, s_far[c] * (SCALE * LOG2E), -1e30) for ok, c in zip(valids, cut[1:])]
            d_parts = [jnp.where(near, d_ref[:, at], d_far[cut[0]])] + [d_far[c] for c in cut[1:]]
            top = functools.reduce(jnp.maximum, [jnp.max(s, axis=0, keepdims=True) for s in s_parts])
            e_parts = [jnp.exp2(s - top) for s in s_parts]
            total = sum(jnp.sum(e, axis=0, keepdims=True) for e in e_parts)
            inv = 1.0 / total
            delta = inv * sum(jnp.sum(e * d, axis=0, keepdims=True) for e, d in zip(e_parts, d_parts))
            for e, d, c in zip(e_parts, d_parts, cut):
                prob = e * inv
                p_ref[c, at] = prob.astype(jnp.bfloat16)
                g_ref[c, at] = (prob * (d - delta)).astype(jnp.bfloat16)
        sums = dot(g_ref[:, g * GROUP * rows : (g + 1) * GROUP * rows], indicator, NN) * SCALE
        own_sums = jnp.where(far_sum, 0.0, sums[:rows]).astype(jnp.bfloat16)
        far_sums = jnp.where(far_sum, sums[:rows], 0.0).astype(jnp.bfloat16)
        if reach > 1:
            far_sums = jnp.concatenate([far_sums, sums[rows:].astype(jnp.bfloat16)], axis=0)
        query_bias = dot(own_sums, head(k_ref, g), TN) + dot(far_sums, far_key, TN)
        bias_ref[g * GROUP : (g + 1) * GROUP, :] = query_bias[:GROUP] + query_bias[GROUP : 2 * GROUP]


def grad_kernel(reach, start_ref, q_ref, c_ref, p_ref, g_ref, own_ref, *back_refs):
    rows = q_ref.shape[0]
    kv_feat = KV_HEADS * HEAD_DIM
    order = [reach] + list(range(1, reach))
    spilled = lax.broadcasted_iota(jnp.int32, (rows, HEAD_DIM), 0) < spill_of(start_ref[...])
    low = jnp.where(spilled, 1.0, 0.0).astype(jnp.bfloat16)
    high = jnp.where(spilled, 0.0, 1.0).astype(jnp.bfloat16)
    for g in range(KV_HEADS):
        at = slice(g * GROUP * rows, (g + 1) * GROUP * rows)
        heads = range(g * GROUP, (g + 1) * GROUP)
        for lhs_ref, rhs_ref, scale, base in ((g_ref, q_ref, SCALE, 0), (p_ref, c_ref, 1.0, kv_feat)):
            two = [jnp.concatenate([head(rhs_ref, h) * high, head(rhs_ref, h) * low], axis=1) for h in heads]
            both = dot(lhs_ref[:, at], jnp.concatenate(two, axis=0), NN) * scale
            late, early = both[:, :HEAD_DIM], both[:, HEAD_DIM:]
            to = slice(base + g * HEAD_DIM, base + (g + 1) * HEAD_DIM)
            own_ref[:, to] = (late[:rows] + jnp.where(spilled, early[:rows], 0.0)).astype(jnp.bfloat16)
            back_refs[reach - 1][:, to] = jnp.where(spilled, 0.0, early[:rows]).astype(jnp.bfloat16)
            for i, j in enumerate(order[1:], 1):
                back_refs[j - 1][:, to] = (late + early)[i * rows : (i + 1) * rows].astype(jnp.bfloat16)


def call(kernel, args, outs, flops, scratch=()):
    vmem = pl.BlockSpec(memory_space=pltpu.VMEM)
    return pl.pallas_call(
        kernel,
        out_shape=[jax.ShapeDtypeStruct(*out) for out in outs],
        in_specs=[vmem] * len(args),
        out_specs=[vmem] * len(outs),
        scratch_shapes=scratch,
        compiler_params=pltpu.CompilerParams(vmem_limit_bytes=32 * 1024 * 1024),
        cost_estimate=pl.CostEstimate(flops=flops, bytes_accessed=2 << 20, transcendentals=0),
    )(*args)


def attend(reach, start, query, cotangent, keys, values, far_keys, far_values):
    rows = query.shape[0]
    kv_feat = keys.shape[1]
    unit = 2 * rows * rows * Q_HEADS * HEAD_DIM
    square = ((rows, Q_HEADS * rows), jnp.float32)
    slots = ((reach * rows, Q_HEADS * rows), jnp.bfloat16)
    block = ((rows, 2 * kv_feat), jnp.bfloat16)
    near = call(near_kernel, (start, query, cotangent, keys, values), [square, square, ((8, HEAD_DIM), jnp.float32)], 2 * unit)
    bias, probs, grads = call(
        functools.partial(far_kernel, reach),
        (start, keys, query, cotangent, *near, *far_keys, *far_values),
        [((Q_HEADS + KV_HEADS, HEAD_DIM), jnp.float32), slots, slots],
        3 * reach * unit,
    )
    own, *backs = call(
        functools.partial(grad_kernel, reach), (start, query, cotangent, probs, grads), [block] * (reach + 1), 2 * reach * unit
    )
    return own, *backs, bias


def shift(array, count, by):
    return lax.ppermute(array, AXES, [(i, (i + by) % count) for i in range(count)])


def stages(count, ctx):
    powers = [1 << i for i in range(count.bit_length() - 1)]
    return [ctx] + [p ^ ctx for p in powers if p > ctx] + [p ^ ctx for p in powers if p < ctx]


def exchange(array, step, count):
    return array + lax.ppermute(array, AXES, [(i, i ^ step) for i in range(count)])


def body(query, keys, values, cotangent, doc_lengths):
    rows = query.shape[0]
    kv_feat = keys.shape[1]
    count = lax.axis_size("dp") * lax.axis_size("ctx")
    reach = lax.axis_size("ctx") // 4
    device = lax.axis_index(AXES)
    far_keys = [shift(keys, count, distance) for distance in range(1, reach + 1)]
    far_values = [shift(values, count, distance) for distance in range(1, reach + 1)]
    ends = jnp.cumsum(doc_lengths)
    position = device * rows + jnp.arange(rows, dtype=jnp.int32)
    start = jnp.max(jnp.where(ends[:, None] <= position[None, :], ends[:, None], 0), axis=0)
    start = (start - device * rows)[None, :]
    own, *rest = attend(reach, start, query, cotangent, keys, values, far_keys, far_values)
    *backs, bias = rest
    received = own.astype(jnp.float32)
    for distance in range(1, reach + 1):
        received = received + shift(backs[distance - 1], count, -distance).astype(jnp.float32)
    received = received.astype(jnp.bfloat16)
    steps = stages(count, lax.axis_size("ctx"))
    for i, step in enumerate(steps):
        if i == len(steps) - 1:
            received, bias = lax.optimization_barrier((received, bias))
        bias = exchange(bias, step, count)
    query_bias = bias[:Q_HEADS].reshape(-1)
    value_bias = bias[Q_HEADS:].reshape(-1)
    return (received[:, :kv_feat], received[:, kv_feat:], query_bias, value_bias)


def solution(mesh):
    return jax.shard_map(
        body,
        mesh=mesh,
        in_specs=(P(AXES, None),) * 4 + (P(),),
        out_specs=(P(AXES, None), P(AXES, None), P(), P()),
        check_vma=False,
    )
```

time: 44.7 us -> 35.5 us (0.79)
  waiting for transfers between devices: 24.9 us -> 13.9 us
  local copies, waits for them, and re-layouts: 6.01 us -> 6.9 us
  starting transfers between devices: 8.16 us -> 8.9 us
    ppermute x3, waiting for transfers between devices: 11 us -> 1.9 us  [shift(): lax.ppermute(array, AXES, [(i, (i + by) % count) for i in range(count)])]
    ppermute x3, starting transfers between devices: 4.66 us -> 6.6 us  [shift(): lax.ppermute(array, AXES, [(i, (i + by) % count) for i in range(count)])]
    ppermute x5, waiting for transfers between devices: 13.9 us -> 12 us  [exchange(): lax.ppermute(array, AXES, [(i, i ^ step) for i in range(count)])]
    ppermute x5, starting transfers between devices: 3.5 us -> 2.29 us  [exchange(): lax.ppermute(array, AXES, [(i, i ^ step) for i in range(count)])]
    unnamed x8, local copies, waits for them, and re-layouts: 3.36 us -> 4.25 us
    pallas_call x1 -> x3, Pallas kernels: 4.37 us -> 4.42 us  [call(): pl.pallas_call(kernel, out_shape=[jax.ShapeDtypeStruct(*out) for out in o...]
  transfers between devices with their start and end apart: 8 -> 8, of which waited for: 8 -> 6; matrix products, arithmetic and copies ran while one was open for 5% -> 5% of each run, Pallas kernels for 0% -> 2%
where the time goes in v2:
time: 35.5 us; the launch traced here: 35.2 us
  waiting for transfers between devices  13.9 us (39%)
  starting transfers between devices  8.9 us (25%)
  local copies, waits for them, and re-layouts  6.9 us (19%)
  Pallas kernels  4.42 us (12%)
  between operations  0.71 us (2%)
  other arithmetic  0.4 us (1%)
    ppermute x5, waiting for transfers between devices, exchange(): lax.ppermute(array, AXES, [(i, i ^ step) for i in range(count)])  12 us
    ppermute x3, starting transfers between devices, shift(): lax.ppermute(array, AXES, [(i, (i + by) % count) for i in range(count)])  6.6 us
    pallas_call x3, Pallas kernels, call(): pl.pallas_call(kernel, out_shape=[jax.ShapeDtypeStruct(*out) for out in o...  4.42 us
    unnamed x8, local copies, waits for them, and re-layouts  4.25 us
    ppermute x5, starting transfers between devices, exchange(): lax.ppermute(array, AXES, [(i, i ^ step) for i in range(count)])  2.29 us
    ppermute x3, waiting for transfers between devices, shift(): lax.ppermute(array, AXES, [(i, (i + by) % count) for i in range(count)])  1.9 us
    another operation x1, local copies, waits for them, and re-layouts  0.74 us
    slice x1, local copies, waits for them, and re-layouts, body(): received[:, kv_feat:]  0.72 us
  transfers between devices with their start and end apart: 8, of which 6 were waited for; matrix products, arithmetic and copies ran while one was open for 5% of the time, Pallas kernels for 2%

profile of v2, /device:TPU:0, one launch (start us, length us, event | category | flops | bytes accessed | tf_op | source)
XLA Modules:
  0.0 35.2 jit_solution(9045858637789052787)
XLA Ops:
  0.6 3.1 %collective-permute-start.1 = (bf16[128,512]{1,0:T(8,128)(2,1)}, bf16[128,512]{1,0:T(8,128)(2,1)S(1)}, u32[]{:S(2)}, u32[]{:S(2)}) collective-permute-start(bf16[128,512]{1,0:T(8,128)(2,1)} %v_ref.1), channel_id=1, source_target_pairs={{0,1},{1,2},{2,3},{3,4},{4,5},{5,6},{6,7},{7,8},{8,9},{9,10},{10,1... | collective-permute-start | bytes 393224 | tf_op jit(solution)/shard_map/ppermute | solution.py:163
  3.7 1.6 %collective-permute-start = (bf16[128,512]{1,0:T(8,128)(2,1)}, bf16[128,512]{1,0:T(8,128)(2,1)S(1)}, u32[]{:S(2)}, u32[]{:S(2)}) collective-permute-start(bf16[128,512]{1,0:T(8,128)(2,1)} %k_ref.3), channel_id=1, source_target_pairs={{0,1},{1,2},{2,3},{3,4},{4,5},{5,6},{6,7},{7,8},{8,9},{9,10},{10,1... | collective-permute-start | bytes 393224 | tf_op jit(solution)/shard_map/ppermute | solution.py:163
  5.3 0.7 %copy.11 = s32[64,1]{1,0:T(8,128)S(1)} copy(s32[64,1]{0,1:T(1,128)} %bitcast.7) | data formatting | bytes 512 | tf_op jit(solution)/shard_map/reshape.32
  6.0 0.1 reduce-window.8
  6.1 0.1 reduce
  6.2 0.1 select_reduce_fusion
  6.4 0.0 copy-start
  6.4 1.2 %copy-done = bf16[128,4096]{1,0:T(8,128)(2,1)S(1)} copy-done((bf16[128,4096]{1,0:T(8,128)(2,1)S(1)}, bf16[128,4096]{1,0:T(8,128)(2,1)}, u32[]{:S(2)}) %copy-start) | copy-done | bytes 1048600
  7.6 1.2 %copy-done.1 = bf16[128,4096]{1,0:T(8,128)(2,1)S(1)} copy-done((bf16[128,4096]{1,0:T(8,128)(2,1)S(1)}, bf16[128,4096]{1,0:T(8,128)(2,1)}, u32[]{:S(2)}) %copy-start.1) | copy-done | bytes 1048600
  8.8 0.9 %copy-done.2 = bf16[128,512]{1,0:T(8,128)(2,1)S(1)} copy-done((bf16[128,512]{1,0:T(8,128)(2,1)S(1)}, bf16[128,512]{1,0:T(8,128)(2,1)}, u32[]{:S(2)}) %copy-start.2) | copy-done | bytes 131096
  9.7 0.9 %copy-done.3 = bf16[128,512]{1,0:T(8,128)(2,1)S(1)} copy-done((bf16[128,512]{1,0:T(8,128)(2,1)S(1)}, bf16[128,512]{1,0:T(8,128)(2,1)}, u32[]{:S(2)}) %copy-start.3) | copy-done | bytes 131096
  10.6 0.8 %shard_map.84 = (f32[128,4096]{1,0:T(8,128)S(1)}, f32[128,4096]{1,0:T(8,128)S(1)}, f32[8,128]{1,0:T(8,128)S(1)}) custom-call(s32[1,128]{1,0:T(1,128)S(1)} %subtract_bitcast_fusion.start_ref, bf16[128,4096]{1,0:T(8,128)(2,1)S(1)} %copy-done, bf16[128,4096]{1,0:T(8,128)(2,1)S(1)} %copy-done.1, bf16[128,512]{1,0:T(8,128)(2,1)S(1)} %copy-done.2, ...), custom_call_target="tpu_custom_call" | custom-call | flops 268435456 | bytes 2097152 | tf_op jit(solution)/shard_map/pallas_call | solution.py:131
  11.4 0.0 collective-permute-done.1.refs_1_
  11.4 1.9 %collective-permute-done.refs_0_ = bf16[128,512]{1,0:T(8,128)(2,1)S(1)} collective-permute-done((bf16[128,512]{1,0:T(8,128)(2,1)}, bf16[128,512]{1,0:T(8,128)(2,1)S(1)}, u32[]{:S(2)}, u32[]{:S(2)}) %collective-permute-start) | collective-permute-done | bytes 131104 | tf_op jit(solution)/shard_map/ppermute | solution.py:163
  13.3 2.7 %shard_map.85 = (f32[36,128]{1,0:T(8,128)S(1)}, bf16[128,4096]{1,0:T(8,128)(2,1)S(1)}, bf16[128,4096]{1,0:T(8,128)(2,1)S(1)}) custom-call(s32[1,128]{1,0:T(1,128)S(1)} %subtract_bitcast_fusion.start_ref, bf16[128,512]{1,0:T(8,128)(2,1)S(1)} %copy-done.2, bf16[128,4096]{1,0:T(8,128)(2,1)S(1)} %copy-done, bf16[128,4096]{1,0:T(8,128)(2,1)S(1)} %copy-done.1, ...), custom_call_target="tpu_custom_call" | custom-call | flops 402653184 | bytes 2097152 | tf_op jit(solution)/shard_map/pallas_call | solution.py:131
  16.0 0.9 %shard_map.86 = (bf16[128,1024]{1,0:T(8,128)(2,1)S(1)}, bf16[128,1024]{1,0:T(8,128)(2,1)S(1)}) custom-call(s32[1,128]{1,0:T(1,128)S(1)} %subtract_bitcast_fusion.start_ref, bf16[128,4096]{1,0:T(8,128)(2,1)S(1)} %copy-done, bf16[128,4096]{1,0:T(8,128)(2,1)S(1)} %copy-done.1, bf16[128,4096]{1,0:T(8,128)(2,1)S(1)} %get-tuple-element.17.p_ref, ...), custom_call_target="tpu_custom_call" | custom-call | flops 268435456 | bytes 2097152 | tf_op jit(solution)/shard_map/pallas_call | solution.py:131
  17.0 1.9 %collective-permute-start.2 = (bf16[128,1024]{1,0:T(8,128)(2,1)S(1)}, bf16[128,1024]{1,0:T(8,128)(2,1)S(1)}, u32[]{:S(2)}, u32[]{:S(2)}) collective-permute-start(bf16[128,1024]{1,0:T(8,128)(2,1)S(1)} %get-tuple-element.20), channel_id=1, source_target_pairs={{0,31},{1,0},{2,1},{3,2},{4,3},{5,4},{6,5},{7,6},{8,7},{9,8},{10,9... | collective-permute-start | bytes 786440 | tf_op jit(solution)/shard_map/ppermute | solution.py:163
  18.9 0.0 collective-permute-start.3
  18.9 1.2 %collective-permute-done.3 = f32[36,128]{1,0:T(8,128)S(1)} collective-permute-done((f32[36,128]{1,0:T(8,128)S(1)}, f32[36,128]{1,0:T(8,128)S(1)}, u32[]{:S(2)}, u32[]{:S(2)}) %collective-permute-start.3) | collective-permute-done | bytes 18464 | tf_op jit(solution)/shard_map/ppermute | solution.py:172
  20.1 0.4 %collective-permute-start.4 = (f32[36,128]{1,0:T(8,128)S(1)}, f32[36,128]{1,0:T(8,128)S(1)}, u32[]{:S(2)}, u32[]{:S(2)}) collective-permute-start(f32[36,128]{1,0:T(8,128)S(1)} %add.35), channel_id=1, source_target_pairs={{0,12},{1,13},{2,14},{3,15},{4,8},{5,9},{6,10},{7,11},{8,4},{9,5},... | collective-permute-start | bytes 55304 | tf_op jit(solution)/shard_map/ppermute | solution.py:172
  20.5 2.9 %collective-permute-done.4 = f32[36,128]{1,0:T(8,128)S(1)} collective-permute-done((f32[36,128]{1,0:T(8,128)S(1)}, f32[36,128]{1,0:T(8,128)S(1)}, u32[]{:S(2)}, u32[]{:S(2)}) %collective-permute-start.4) | collective-permute-done | bytes 18464 | tf_op jit(solution)/shard_map/ppermute | solution.py:172
  23.3 1.6 %collective-permute-start.5 = (f32[36,128]{1,0:T(8,128)S(1)}, f32[36,128]{1,0:T(8,128)S(1)}, u32[]{:S(2)}, u32[]{:S(2)}) collective-permute-start(f32[36,128]{1,0:T(8,128)S(1)} %add.36), channel_id=1, source_target_pairs={{0,20},{1,21},{2,22},{3,23},{4,16},{5,17},{6,18},{7,19},{8,28},{9,... | collective-permute-start | bytes 55304 | tf_op jit(solution)/shard_map/ppermute | solution.py:172
  24.9 1.6 %collective-permute-done.5 = f32[36,128]{1,0:T(8,128)S(1)} collective-permute-done((f32[36,128]{1,0:T(8,128)S(1)}, f32[36,128]{1,0:T(8,128)S(1)}, u32[]{:S(2)}, u32[]{:S(2)}) %collective-permute-start.5) | collective-permute-done | bytes 18464 | tf_op jit(solution)/shard_map/ppermute | solution.py:172
  26.5 0.3 collective-permute-start.6
  26.8 2.9 %collective-permute-done.6 = f32[36,128]{1,0:T(8,128)S(1)} collective-permute-done((f32[36,128]{1,0:T(8,128)S(1)}, f32[36,128]{1,0:T(8,128)S(1)}, u32[]{:S(2)}, u32[]{:S(2)}) %collective-permute-start.6) | collective-permute-done | bytes 18464 | tf_op jit(solution)/shard_map/ppermute | solution.py:172
  29.7 0.0 collective-permute-done.2
  29.8 0.1 add_convert_fusion
  29.8 0.1 collective-permute-start.7
  29.9 0.7 %fusion = (bf16[128,512]{1,0:T(8,128)(2,1)}, bf16[128,512]{1,0:T(8,128)(2,1)}) fusion(bf16[128,1024]{1,0:T(8,128)(2,1)S(1)} %add_convert_fusion), kind=kLoop, calls=%fused_computation.6 | loop fusion | bytes 524288 | tf_op jit(solution)/shard_map/slice | solution.py:200
  30.6 3.4 %collective-permute-done.7 = f32[36,128]{1,0:T(8,128)S(1)} collective-permute-done((f32[36,128]{1,0:T(8,128)S(1)}, f32[36,128]{1,0:T(8,128)S(1)}, u32[]{:S(2)}, u32[]{:S(2)}) %collective-permute-start.7) | collective-permute-done | bytes 18464 | tf_op jit(solution)/shard_map/ppermute | solution.py:172
  34.1 0.6 %slice_bitcast_fusion.1 = f32[512]{0:T(512)} fusion(f32[36,128]{1,0:T(8,128)S(1)} %add.39), kind=kLoop, calls=%fused_computation.3 | loop fusion | bytes 4096 | tf_op jit(solution)/shard_map/reshape | solution.py:199
  34.6 0.6 %slice_bitcast_fusion = f32[4096]{0:T(1024)} fusion(f32[36,128]{1,0:T(8,128)S(1)} %add.39), kind=kLoop, calls=%fused_computation.2 | loop fusion | bytes 32768 | tf_op jit(solution)/shard_map/reshape | solution.py:198
  (10 shorter events, 0.0 us)
Async XLA Ops:
  0.6 10.8 %collective-permute-start.1 = (bf16[128,512]{1,0:T(8,128)(2,1)}, bf16[128,512]{1,0:T(8,128)(2,1)S(1)}, u32[]{:S(2)}, u32[]{:S(2)}) collective-permute-start(bf16[128,512]{1,0:T(8,128)(2,1)} %v_ref.1), channel_id=1, source_target_pairs={{0,1},{1,2},{2,3},{3,4},{4,5},{5,6},{6,7},{7,8},{8,9},{9,10},{10,1... | collective-permute-start | bytes 393224 | tf_op jit(solution)/shard_map/ppermute | solution.py:163
  3.7 9.6 %collective-permute-start = (bf16[128,512]{1,0:T(8,128)(2,1)}, bf16[128,512]{1,0:T(8,128)(2,1)S(1)}, u32[]{:S(2)}, u32[]{:S(2)}) collective-permute-start(bf16[128,512]{1,0:T(8,128)(2,1)} %k_ref.3), channel_id=1, source_target_pairs={{0,1},{1,2},{2,3},{3,4},{4,5},{5,6},{6,7},{7,8},{8,9},{9,10},{10,1... | collective-permute-start | bytes 393224 | tf_op jit(solution)/shard_map/ppermute | solution.py:163
  6.4 1.2 %copy-start = (bf16[128,4096]{1,0:T(8,128)(2,1)S(1)}, bf16[128,4096]{1,0:T(8,128)(2,1)}, u32[]{:S(2)}) copy-start(bf16[128,4096]{1,0:T(8,128)(2,1)} %q_ref.5) | copy-start | bytes 3145732
  7.6 1.2 %copy-start.1 = (bf16[128,4096]{1,0:T(8,128)(2,1)S(1)}, bf16[128,4096]{1,0:T(8,128)(2,1)}, u32[]{:S(2)}) copy-start(bf16[128,4096]{1,0:T(8,128)(2,1)} %c_ref.5) | copy-start | bytes 3145732
  8.8 0.9 %copy-start.2 = (bf16[128,512]{1,0:T(8,128)(2,1)S(1)}, bf16[128,512]{1,0:T(8,128)(2,1)}, u32[]{:S(2)}) copy-start(bf16[128,512]{1,0:T(8,128)(2,1)} %k_ref.3) | copy-start | bytes 393220
  9.7 0.9 %copy-start.3 = (bf16[128,512]{1,0:T(8,128)(2,1)S(1)}, bf16[128,512]{1,0:T(8,128)(2,1)}, u32[]{:S(2)}) copy-start(bf16[128,512]{1,0:T(8,128)(2,1)} %v_ref.1) | copy-start | bytes 393220
  17.0 12.8 %collective-permute-start.2 = (bf16[128,1024]{1,0:T(8,128)(2,1)S(1)}, bf16[128,1024]{1,0:T(8,128)(2,1)S(1)}, u32[]{:S(2)}, u32[]{:S(2)}) collective-permute-start(bf16[128,1024]{1,0:T(8,128)(2,1)S(1)} %get-tuple-element.20), channel_id=1, source_target_pairs={{0,31},{1,0},{2,1},{3,2},{4,3},{5,4},{6,5},{7,6},{8,7},{9,8},{10,9... | collective-permute-start | bytes 786440 | tf_op jit(solution)/shard_map/ppermute | solution.py:163
  18.9 1.2 %collective-permute-start.3 = (f32[36,128]{1,0:T(8,128)S(1)}, f32[36,128]{1,0:T(8,128)S(1)}, u32[]{:S(2)}, u32[]{:S(2)}) collective-permute-start(f32[36,128]{1,0:T(8,128)S(1)} %get-tuple-element.21), channel_id=1, source_target_pairs={{0,4},{1,5},{2,6},{3,7},{4,0},{5,1},{6,2},{7,3},{8,12},{9,13},{10,... | collective-permute-start | bytes 55304 | tf_op jit(solution)/shard_map/ppermute | solution.py:172
  20.1 3.2 %collective-permute-start.4 = (f32[36,128]{1,0:T(8,128)S(1)}, f32[36,128]{1,0:T(8,128)S(1)}, u32[]{:S(2)}, u32[]{:S(2)}) collective-permute-start(f32[36,128]{1,0:T(8,128)S(1)} %add.35), channel_id=1, source_target_pairs={{0,12},{1,13},{2,14},{3,15},{4,8},{5,9},{6,10},{7,11},{8,4},{9,5},... | collective-permute-start | bytes 55304 | tf_op jit(solution)/shard_map/ppermute | solution.py:172
  23.3 3.2 %collective-permute-start.5 = (f32[36,128]{1,0:T(8,128)S(1)}, f32[36,128]{1,0:T(8,128)S(1)}, u32[]{:S(2)}, u32[]{:S(2)}) collective-permute-start(f32[36,128]{1,0:T(8,128)S(1)} %add.36), channel_id=1, source_target_pairs={{0,20},{1,21},{2,22},{3,23},{4,16},{5,17},{6,18},{7,19},{8,28},{9,... | collective-permute-start | bytes 55304 | tf_op jit(solution)/shard_map/ppermute | solution.py:172
  26.5 3.2 %collective-permute-start.6 = (f32[36,128]{1,0:T(8,128)S(1)}, f32[36,128]{1,0:T(8,128)S(1)}, u32[]{:S(2)}, u32[]{:S(2)}) collective-permute-start(f32[36,128]{1,0:T(8,128)S(1)} %add.37), channel_id=1, source_target_pairs={{0,5},{1,4},{2,7},{3,6},{4,1},{5,0},{6,3},{7,2},{8,13},{9,12},{10,... | collective-permute-start | bytes 55304 | tf_op jit(solution)/shard_map/ppermute | solution.py:172
  29.8 4.2 %collective-permute-start.7 = (f32[36,128]{1,0:T(8,128)S(1)}, f32[36,128]{1,0:T(8,128)S(1)}, u32[]{:S(2)}, u32[]{:S(2)}) collective-permute-start(f32[36,128]{1,0:T(8,128)S(1)} %add.38), channel_id=1, source_target_pairs={{0,6},{1,7},{2,4},{3,5},{4,2},{5,3},{6,0},{7,1},{8,14},{9,15},{10,... | collective-permute-start | bytes 55304 | tf_op jit(solution)/shard_map/ppermute | solution.py:172

commit v3 on v2

--- a/solution.py
+++ b/solution.py
@@ -56,8 +56,8 @@
 
 
 def far_kernel(reach, start_ref, k_ref, q_ref, c_ref, s_ref, d_ref, sum_ref, *refs):
-    kp_refs, vp_refs = refs[:reach], refs[reach : 2 * reach]
-    bias_ref, p_ref, g_ref = refs[2 * reach :]
+    *far_refs, bias_ref, p_ref, g_ref = refs
+    kp_refs, vp_refs = far_refs[::2], far_refs[1::2]
     rows = q_ref.shape[0]
     wide = 2 * rows
     key_row, near = grids(rows, wide)
@@ -139,7 +139,7 @@
     )(*args)
 
 
-def attend(reach, start, query, cotangent, keys, values, far_keys, far_values):
+def attend(reach, start, query, cotangent, keys, values, far):
     rows = query.shape[0]
     kv_feat = keys.shape[1]
     unit = 2 * rows * rows * Q_HEADS * HEAD_DIM
@@ -149,27 +149,86 @@
     near = call(near_kernel, (start, query, cotangent, keys, values), [square, square, ((8, HEAD_DIM), jnp.float32)], 2 * unit)
     bias, probs, grads = call(
         functools.partial(far_kernel, reach),
-        (start, keys, query, cotangent, *near, *far_keys, *far_values),
+        (start, keys, query, cotangent, *near, *far),
         [((Q_HEADS + KV_HEADS, HEAD_DIM), jnp.float32), slots, slots],
         3 * reach * unit,
     )
-    own, *backs = call(
-        functools.partial(grad_kernel, reach), (start, query, cotangent, probs, grads), [block] * (reach + 1), 2 * reach * unit
-    )
-    return own, *backs, bias
+
+    def gradients(start):
+        return call(
+            functools.partial(grad_kernel, reach), (start, query, cotangent, probs, grads), [block] * (reach + 1), 2 * reach * unit
+        )
+
+    return bias, gradients
 
 
 def shift(array, count, by):
     return lax.ppermute(array, AXES, [(i, (i + by) % count) for i in range(count)])
 
 
+EXCHANGE_FLOPS = 2360_000_000
+
+
 def stages(count, ctx):
     powers = [1 << i for i in range(count.bit_length() - 1)]
-    return [ctx] + [p ^ ctx for p in powers if p > ctx] + [p ^ ctx for p in powers if p < ctx]
-
-
-def exchange(array, step, count):
-    return array + lax.ppermute(array, AXES, [(i, i ^ step) for i in range(count)])
+    masks = [[ctx]] + [[p ^ ctx] for p in powers if p > ctx]
+    inner = [p for p in powers if p < ctx]
+    for i in range(0, len(inner), 2):
+        pair = inner[i : i + 2]
+        masks.append([p ^ ctx for p in pair] + ([pair[0] ^ pair[1] ^ ctx] if len(pair) > 1 else []))
+    return masks
+
+
+def exchange(array, masks, count):
+    got = [lax.ppermute(array, AXES, [(i, i ^ mask) for i in range(count)]) for mask in masks]
+    return [array] + got
+
+
+def total_of(terms):
+    while len(terms) > 1:
+        terms = [functools.reduce(jnp.add, terms[i : i + 2]) for i in range(0, len(terms), 2)]
+    return terms[0]
+
+
+def add_kernel(*refs):
+    *term_refs, out_ref = refs
+    out_ref[...] = total_of([ref[...] for ref in term_refs])
+
+
+def add(terms):
+    return call(add_kernel, terms, [(terms[0].shape, terms[0].dtype)], EXCHANGE_FLOPS)[0]
+
+
+def last_kernel(n_terms, n_parts, *refs):
+    term_refs, part_refs = refs[:n_terms], refs[n_terms : n_terms + n_parts]
+    outs, bufs, sems = refs[n_terms + n_parts : -5], refs[-5:-1], refs[-1]
+    total = total_of([ref[...] for ref in term_refs])
+    kv_feat = bufs[2].shape[1]
+    copies = [pltpu.make_async_copy(bufs[i], outs[i], sems.at[i]) for i in range(4)]
+    bufs[0][...] = total[:Q_HEADS]
+    copies[0].start()
+    bufs[1][...] = total[Q_HEADS:]
+    copies[1].start()
+    for i in range(2):
+        cols = slice(i * kv_feat, (i + 1) * kv_feat)
+        grad = functools.reduce(jnp.add, [ref[:, cols].astype(jnp.float32) for ref in part_refs])
+        bufs[2 + i][...] = grad.astype(jnp.bfloat16)
+        copies[2 + i].start()
+    for copy in copies:
+        copy.wait()
+
+
+def last(terms, parts):
+    rows, feat = parts[0].shape
+    shapes = [((Q_HEADS, HEAD_DIM), jnp.float32), ((KV_HEADS, HEAD_DIM), jnp.float32)] + [((rows, feat // 2), jnp.bfloat16)] * 2
+    return pl.pallas_call(
+        functools.partial(last_kernel, len(terms), len(parts)),
+        out_shape=[jax.ShapeDtypeStruct(*shape) for shape in shapes],
+        in_specs=[pl.BlockSpec(memory_space=pltpu.VMEM)] * (len(terms) + len(parts)),
+        out_specs=[pl.BlockSpec(memory_space=pl.ANY)] * 4,
+        scratch_shapes=[pltpu.VMEM(*shape) for shape in shapes] + [pltpu.SemaphoreType.DMA((4,))],
+        compiler_params=pltpu.CompilerParams(vmem_limit_bytes=8 * 1024 * 1024),
+    )(*terms, *parts)
 
 
 def body(query, keys, values, cotangent, doc_lengths):
@@ -178,26 +237,23 @@
     count = lax.axis_size("dp") * lax.axis_size("ctx")
     reach = lax.axis_size("ctx") // 4
     device = lax.axis_index(AXES)
-    far_keys = [shift(keys, count, distance) for distance in range(1, reach + 1)]
-    far_values = [shift(values, count, distance) for distance in range(1, reach + 1)]
+    far = [shift(x, count, distance) for distance in range(1, reach + 1) for x in (keys, values)]
     ends = jnp.cumsum(doc_lengths)
     position = device * rows + jnp.arange(rows, dtype=jnp.int32)
     start = jnp.max(jnp.where(ends[:, None] <= position[None, :], ends[:, None], 0), axis=0)
     start = (start - device * rows)[None, :]
-    own, *rest = attend(reach, start, query, cotangent, keys, values, far_keys, far_values)
-    *backs, bias = rest
-    received = own.astype(jnp.float32)
-    for distance in range(1, reach + 1):
-        received = received + shift(backs[distance - 1], count, -distance).astype(jnp.float32)
-    received = received.astype(jnp.bfloat16)
+    bias, gradients = attend(reach, start, query, cotangent, keys, values, far)
     steps = stages(count, lax.axis_size("ctx"))
-    for i, step in enumerate(steps):
-        if i == len(steps) - 1:
-            received, bias = lax.optimization_barrier((received, bias))
-        bias = exchange(bias, step, count)
-    query_bias = bias[:Q_HEADS].reshape(-1)
-    value_bias = bias[Q_HEADS:].reshape(-1)
-    return (received[:, :kv_feat], received[:, kv_feat:], query_bias, value_bias)
+    parts = None
+    for i, masks in enumerate(steps):
+        if i == 1:
+            start, bias = lax.optimization_barrier((start, bias))
+            own, *backs = gradients(start)
+            parts = [own] + [shift(backs[distance - 1], count, -distance) for distance in range(1, reach + 1)]
+        terms = exchange(bias, masks, count)
+        bias = add(terms) if i == 2 else total_of(terms)
+    query_bias, value_bias, key_grad, value_grad = last(terms, parts)
+    return (key_grad, value_grad, query_bias.reshape(-1), value_bias.reshape(-1))
 
 
 def solution(mesh):

time: 35.5 us -> 31.2 us (0.88)
  waiting for transfers between devices: 13.9 us -> 7.28 us
  starting transfers between devices: 8.9 us -> 12.5 us
  local copies, waits for them, and re-layouts: 6.9 us -> 5 us
  Pallas kernels: 4.42 us -> 5.18 us
    ppermute x5 -> x6, waiting for transfers between devices: 12 us -> 5.38 us  [exchange(): lax.ppermute(array, AXES, [(i, i ^ mask) for i in range(count)])]
    ppermute x5 -> x6, starting transfers between devices: 2.29 us -> 5.57 us  [exchange(): lax.ppermute(array, AXES, [(i, i ^ mask) for i in range(count)])]
    reshape x2 -> x0, local copies, waits for them, and re-layouts: 1.19 us -> none  [the longest x1 0.61 us: body(): query_bias = bias[:Q_HEADS].reshape(-1)]
    pallas_call x0 -> x1, Pallas kernels: none -> 0.77 us  [last(): pl.pallas_call(functools.partial(last_kernel, len(terms), len(parts)), ou...]
    slice x1 -> x0, local copies, waits for them, and re-layouts: 0.72 us -> none  [body(): received[:, kv_feat:]]
    pallas_call x3 -> x4, Pallas kernels: 4.42 us -> 4.41 us  [call(): pl.pallas_call(kernel, out_shape=[jax.ShapeDtypeStruct(*out) for out in o...]
  transfers between devices with their start and end apart: 8 -> 9, of which waited for: 6 -> 5; matrix products, arithmetic and copies ran while one was open for 5% -> 3% of each run, Pallas kernels for 2% -> 6%
where the time goes in v3:
time: 31.2 us; the launch traced here: 30.9 us
  starting transfers between devices  12.5 us (40%)
  waiting for transfers between devices  7.28 us (23%)
  Pallas kernels  5.18 us (17%)
  local copies, waits for them, and re-layouts  5 us (16%)
  between operations  0.7 us (2%)
  other arithmetic  0.32 us (1%)
    ppermute x3, starting transfers between devices, shift(): lax.ppermute(array, AXES, [(i, (i + by) % count) for i in range(count)])  6.9 us
    ppermute x6, starting transfers between devices, exchange(): lax.ppermute(array, AXES, [(i, i ^ mask) for i in range(count)])  5.57 us
    ppermute x6, waiting for transfers between devices, exchange(): lax.ppermute(array, AXES, [(i, i ^ mask) for i in range(count)])  5.38 us
    pallas_call x4, Pallas kernels, call(): pl.pallas_call(kernel, out_shape=[jax.ShapeDtypeStruct(*out) for out in o...  4.41 us
    unnamed x8, local copies, waits for them, and re-layouts  4.25 us
    ppermute x3, waiting for transfers between devices, shift(): lax.ppermute(array, AXES, [(i, (i + by) % count) for i in range(count)])  1.9 us
    pallas_call x1, Pallas kernels, last(): pl.pallas_call(functools.partial(last_kernel, len(terms), len(parts)), ou...  0.77 us
    another operation x1, local copies, waits for them, and re-layouts  0.74 us
  transfers between devices with their start and end apart: 9, of which 5 were waited for; matrix products, arithmetic and copies ran while one was open for 3% of the time, Pallas kernels for 6%

profile of v3, /device:TPU:0, one launch (start us, length us, event | category | flops | bytes accessed | tf_op | source)
XLA Modules:
  0.0 30.9 jit_solution(9006671209711495202)
XLA Ops:
  0.6 3.1 %collective-permute-start.1 = (bf16[128,512]{1,0:T(8,128)(2,1)}, bf16[128,512]{1,0:T(8,128)(2,1)S(1)}, u32[]{:S(2)}, u32[]{:S(2)}) collective-permute-start(bf16[128,512]{1,0:T(8,128)(2,1)} %v_ref.1), channel_id=1, source_target_pairs={{0,1},{1,2},{2,3},{3,4},{4,5},{5,6},{6,7},{7,8},{8,9},{9,10},{10,1... | collective-permute-start | bytes 393224 | tf_op jit(solution)/shard_map/ppermute | solution.py:166
  3.7 1.6 %collective-permute-start = (bf16[128,512]{1,0:T(8,128)(2,1)}, bf16[128,512]{1,0:T(8,128)(2,1)S(1)}, u32[]{:S(2)}, u32[]{:S(2)}) collective-permute-start(bf16[128,512]{1,0:T(8,128)(2,1)} %k_ref.3), channel_id=1, source_target_pairs={{0,1},{1,2},{2,3},{3,4},{4,5},{5,6},{6,7},{7,8},{8,9},{9,10},{10,1... | collective-permute-start | bytes 393224 | tf_op jit(solution)/shard_map/ppermute | solution.py:166
  5.3 0.7 %copy.11 = s32[64,1]{1,0:T(8,128)S(1)} copy(s32[64,1]{0,1:T(1,128)} %bitcast.5) | data formatting | bytes 512 | tf_op jit(solution)/shard_map/reshape.32
  6.0 0.1 reduce-window.8
  6.1 0.1 reduce
  6.2 0.1 select_reduce_fusion
  6.4 0.0 copy-start
  6.4 1.2 %copy-done = bf16[128,4096]{1,0:T(8,128)(2,1)S(1)} copy-done((bf16[128,4096]{1,0:T(8,128)(2,1)S(1)}, bf16[128,4096]{1,0:T(8,128)(2,1)}, u32[]{:S(2)}) %copy-start) | copy-done | bytes 1048600
  7.6 0.0 copy-start.1
  7.6 1.2 %copy-done.1 = bf16[128,4096]{1,0:T(8,128)(2,1)S(1)} copy-done((bf16[128,4096]{1,0:T(8,128)(2,1)S(1)}, bf16[128,4096]{1,0:T(8,128)(2,1)}, u32[]{:S(2)}) %copy-start.1) | copy-done | bytes 1048600
  8.8 0.9 %copy-done.2 = bf16[128,512]{1,0:T(8,128)(2,1)S(1)} copy-done((bf16[128,512]{1,0:T(8,128)(2,1)S(1)}, bf16[128,512]{1,0:T(8,128)(2,1)}, u32[]{:S(2)}) %copy-start.2) | copy-done | bytes 131096
  9.7 0.9 %copy-done.3 = bf16[128,512]{1,0:T(8,128)(2,1)S(1)} copy-done((bf16[128,512]{1,0:T(8,128)(2,1)S(1)}, bf16[128,512]{1,0:T(8,128)(2,1)}, u32[]{:S(2)}) %copy-start.3) | copy-done | bytes 131096
  10.6 0.8 %shard_map.84 = (f32[128,4096]{1,0:T(8,128)S(1)}, f32[128,4096]{1,0:T(8,128)S(1)}, f32[8,128]{1,0:T(8,128)S(1)}) custom-call(s32[1,128]{1,0:T(1,128)S(1)} %subtract_bitcast_fusion.start_ref, bf16[128,4096]{1,0:T(8,128)(2,1)S(1)} %copy-done, bf16[128,4096]{1,0:T(8,128)(2,1)S(1)} %copy-done.1, bf16[128,512]{1,0:T(8,128)(2,1)S(1)} %copy-done.2, ...), custom_call_target="tpu_custom_call" | custom-call | flops 268435456 | bytes 2097152 | tf_op jit(solution)/shard_map/pallas_call | solution.py:131
  11.4 0.0 collective-permute-done.1.refs_1_
  11.4 1.9 %collective-permute-done.refs_0_ = bf16[128,512]{1,0:T(8,128)(2,1)S(1)} collective-permute-done((bf16[128,512]{1,0:T(8,128)(2,1)}, bf16[128,512]{1,0:T(8,128)(2,1)S(1)}, u32[]{:S(2)}, u32[]{:S(2)}) %collective-permute-start) | collective-permute-done | bytes 131104 | tf_op jit(solution)/shard_map/ppermute | solution.py:166
  13.3 2.7 %shard_map.85 = (f32[36,128]{1,0:T(8,128)S(1)}, bf16[128,4096]{1,0:T(8,128)(2,1)S(1)}, bf16[128,4096]{1,0:T(8,128)(2,1)S(1)}) custom-call(s32[1,128]{1,0:T(1,128)S(1)} %subtract_bitcast_fusion.start_ref, bf16[128,512]{1,0:T(8,128)(2,1)S(1)} %copy-done.2, bf16[128,4096]{1,0:T(8,128)(2,1)S(1)} %copy-done, bf16[128,4096]{1,0:T(8,128)(2,1)S(1)} %copy-done.1, ...), custom_call_target="tpu_custom_call" | custom-call | flops 402653184 | bytes 2097152 | tf_op jit(solution)/shard_map/pallas_call | solution.py:131
  16.0 0.1 collective-permute-start.2
  16.1 1.2 %collective-permute-done.2 = f32[36,128]{1,0:T(8,128)S(1)} collective-permute-done((f32[36,128]{1,0:T(8,128)S(1)}, f32[36,128]{1,0:T(8,128)S(1)}, u32[]{:S(2)}, u32[]{:S(2)}) %collective-permute-start.2) | collective-permute-done | bytes 18464 | tf_op jit(solution)/shard_map/ppermute | solution.py:183
  17.3 1.0 %collective-permute-start.3 = (f32[36,128]{1,0:T(8,128)S(1)}, f32[36,128]{1,0:T(8,128)S(1)}, u32[]{:S(2)}, u32[]{:S(2)}) collective-permute-start(f32[36,128]{1,0:T(8,128)S(1)} %add.22), channel_id=1, source_target_pairs={{0,12},{1,13},{2,14},{3,15},{4,8},{5,9},{6,10},{7,11},{8,4},{9,5},... | collective-permute-start | bytes 55304 | tf_op jit(solution)/shard_map/ppermute | solution.py:183
  18.3 0.9 %shard_map.87 = (bf16[128,1024]{1,0:T(8,128)(2,1)S(1)}, bf16[128,1024]{1,0:T(8,128)(2,1)S(1)}) custom-call(s32[1,128]{1,0:T(1,128)S(1)} %subtract_bitcast_fusion.start_ref, bf16[128,4096]{1,0:T(8,128)(2,1)S(1)} %copy-done, bf16[128,4096]{1,0:T(8,128)(2,1)S(1)} %copy-done.1, bf16[128,4096]{1,0:T(8,128)(2,1)S(1)} %get-tuple-element.24.p_ref, ...), custom_call_target="tpu_custom_call" | custom-call | flops 268435456 | bytes 2097152 | tf_op jit(solution)/shard_map/pallas_call | solution.py:131
  19.2 2.2 %collective-permute-start.8 = (bf16[128,1024]{1,0:T(8,128)(2,1)S(1)}, bf16[128,1024]{1,0:T(8,128)(2,1)S(1)}, u32[]{:S(2)}, u32[]{:S(2)}) collective-permute-start(bf16[128,1024]{1,0:T(8,128)(2,1)S(1)} %get-tuple-element.27), channel_id=1, source_target_pairs={{0,31},{1,0},{2,1},{3,2},{4,3},{5,4},{6,5},{7,6},{8,7},{9,8},{10,9... | collective-permute-start | bytes 786440 | tf_op jit(solution)/shard_map/ppermute | solution.py:166
  21.5 0.0 collective-permute-done.3
  21.5 1.0 %collective-permute-start.4 = (f32[36,128]{1,0:T(8,128)S(1)}, f32[36,128]{1,0:T(8,128)S(1)}, u32[]{:S(2)}, u32[]{:S(2)}) collective-permute-start(f32[36,128]{1,0:T(8,128)S(1)} %add.23.refs_0_), channel_id=1, source_target_pairs={{0,20},{1,21},{2,22},{3,23},{4,16},{5,17},{6,18},{7,19},{8,28},{9,... | collective-permute-start | bytes 55304 | tf_op jit(solution)/shard_map/ppermute | solution.py:183
  22.4 2.3 %collective-permute-done.4.refs_1_ = f32[36,128]{1,0:T(8,128)S(1)} collective-permute-done((f32[36,128]{1,0:T(8,128)S(1)}, f32[36,128]{1,0:T(8,128)S(1)}, u32[]{:S(2)}, u32[]{:S(2)}) %collective-permute-start.4) | collective-permute-done | bytes 18464 | tf_op jit(solution)/shard_map/ppermute | solution.py:183
  24.7 0.0 collective-permute-start.7
  24.8 1.0 %collective-permute-start.6 = (f32[36,128]{1,0:T(8,128)S(1)}, f32[36,128]{1,0:T(8,128)S(1)}, u32[]{:S(2)}, u32[]{:S(2)}) collective-permute-start(f32[36,128]{1,0:T(8,128)S(1)} %shard_map.86.refs_0_), channel_id=1, source_target_pairs={{0,6},{1,7},{2,4},{3,5},{4,2},{5,3},{6,0},{7,1},{8,14},{9,15},{10,... | collective-permute-start | bytes 55304 | tf_op jit(solution)/shard_map/ppermute | solution.py:183
  25.8 2.5 %collective-permute-start.5 = (f32[36,128]{1,0:T(8,128)S(1)}, f32[36,128]{1,0:T(8,128)S(1)}, u32[]{:S(2)}, u32[]{:S(2)}) collective-permute-start(f32[36,128]{1,0:T(8,128)S(1)} %shard_map.86.refs_0_), channel_id=1, source_target_pairs={{0,5},{1,4},{2,7},{3,6},{4,1},{5,0},{6,3},{7,2},{8,13},{9,12},{10,... | collective-permute-start | bytes 55304 | tf_op jit(solution)/shard_map/ppermute | solution.py:183
  28.3 1.8 %collective-permute-done.7.refs_3_ = f32[36,128]{1,0:T(8,128)S(1)} collective-permute-done((f32[36,128]{1,0:T(8,128)S(1)}, f32[36,128]{1,0:T(8,128)S(1)}, u32[]{:S(2)}, u32[]{:S(2)}) %collective-permute-start.7) | collective-permute-done | bytes 18464 | tf_op jit(solution)/shard_map/ppermute | solution.py:183
  30.1 0.0 collective-permute-done.6.refs_2_
  30.1 0.1 collective-permute-done.5.refs_1_
  30.2 0.0 collective-permute-done.8.refs_5_
  30.2 0.8 %shard_map.88 = (f32[32,128]{1,0:T(8,128)}, f32[4,128]{1,0:T(4,128)}, bf16[128,512]{1,0:T(8,128)(2,1)}, bf16[128,512]{1,0:T(8,128)(2,1)}) custom-call(f32[36,128]{1,0:T(8,128)S(1)} %shard_map.86.refs_0_, f32[36,128]{1,0:T(8,128)S(1)} %collective-permute-done.5.refs_1_, f32[36,128]{1,0:T(8,128)S(1)} %collective-permute-done.6.refs_2_, ...), custom_call_target="tpu_custom_call" | custom-call | tf_op jit(solution)/shard_map/pallas_call | solution.py:224
  (7 shorter events, 0.0 us)
Async XLA Ops:
  0.6 10.8 %collective-permute-start.1 = (bf16[128,512]{1,0:T(8,128)(2,1)}, bf16[128,512]{1,0:T(8,128)(2,1)S(1)}, u32[]{:S(2)}, u32[]{:S(2)}) collective-permute-start(bf16[128,512]{1,0:T(8,128)(2,1)} %v_ref.1), channel_id=1, source_target_pairs={{0,1},{1,2},{2,3},{3,4},{4,5},{5,6},{6,7},{7,8},{8,9},{9,10},{10,1... | collective-permute-start | bytes 393224 | tf_op jit(solution)/shard_map/ppermute | solution.py:166
  3.7 9.6 %collective-permute-start = (bf16[128,512]{1,0:T(8,128)(2,1)}, bf16[128,512]{1,0:T(8,128)(2,1)S(1)}, u32[]{:S(2)}, u32[]{:S(2)}) collective-permute-start(bf16[128,512]{1,0:T(8,128)(2,1)} %k_ref.3), channel_id=1, source_target_pairs={{0,1},{1,2},{2,3},{3,4},{4,5},{5,6},{6,7},{7,8},{8,9},{9,10},{10,1... | collective-permute-start | bytes 393224 | tf_op jit(solution)/shard_map/ppermute | solution.py:166
  6.4 1.2 %copy-start = (bf16[128,4096]{1,0:T(8,128)(2,1)S(1)}, bf16[128,4096]{1,0:T(8,128)(2,1)}, u32[]{:S(2)}) copy-start(bf16[128,4096]{1,0:T(8,128)(2,1)} %q_ref.5) | copy-start | bytes 3145732
  7.6 1.2 %copy-start.1 = (bf16[128,4096]{1,0:T(8,128)(2,1)S(1)}, bf16[128,4096]{1,0:T(8,128)(2,1)}, u32[]{:S(2)}) copy-start(bf16[128,4096]{1,0:T(8,128)(2,1)} %c_ref.5) | copy-start | bytes 3145732
  8.8 0.9 %copy-start.2 = (bf16[128,512]{1,0:T(8,128)(2,1)S(1)}, bf16[128,512]{1,0:T(8,128)(2,1)}, u32[]{:S(2)}) copy-start(bf16[128,512]{1,0:T(8,128)(2,1)} %k_ref.3) | copy-start | bytes 393220
  9.7 0.9 %copy-start.3 = (bf16[128,512]{1,0:T(8,128)(2,1)S(1)}, bf16[128,512]{1,0:T(8,128)(2,1)}, u32[]{:S(2)}) copy-start(bf16[128,512]{1,0:T(8,128)(2,1)} %v_ref.1) | copy-start | bytes 393220
  16.0 1.3 %collective-permute-start.2 = (f32[36,128]{1,0:T(8,128)S(1)}, f32[36,128]{1,0:T(8,128)S(1)}, u32[]{:S(2)}, u32[]{:S(2)}) collective-permute-start(f32[36,128]{1,0:T(8,128)S(1)} %get-tuple-element.21), channel_id=1, source_target_pairs={{0,4},{1,5},{2,6},{3,7},{4,0},{5,1},{6,2},{7,3},{8,12},{9,13},{10,... | collective-permute-start | bytes 55304 | tf_op jit(solution)/shard_map/ppermute | solution.py:183
  17.3 4.2 %collective-permute-start.3 = (f32[36,128]{1,0:T(8,128)S(1)}, f32[36,128]{1,0:T(8,128)S(1)}, u32[]{:S(2)}, u32[]{:S(2)}) collective-permute-start(f32[36,128]{1,0:T(8,128)S(1)} %add.22), channel_id=1, source_target_pairs={{0,12},{1,13},{2,14},{3,15},{4,8},{5,9},{6,10},{7,11},{8,4},{9,5},... | collective-permute-start | bytes 55304 | tf_op jit(solution)/shard_map/ppermute | solution.py:183
  19.2 11.0 %collective-permute-start.8 = (bf16[128,1024]{1,0:T(8,128)(2,1)S(1)}, bf16[128,1024]{1,0:T(8,128)(2,1)S(1)}, u32[]{:S(2)}, u32[]{:S(2)}) collective-permute-start(bf16[128,1024]{1,0:T(8,128)(2,1)S(1)} %get-tuple-element.27), channel_id=1, source_target_pairs={{0,31},{1,0},{2,1},{3,2},{4,3},{5,4},{6,5},{7,6},{8,7},{9,8},{10,9... | collective-permute-start | bytes 786440 | tf_op jit(solution)/shard_map/ppermute | solution.py:166
  21.5 3.3 %collective-permute-start.4 = (f32[36,128]{1,0:T(8,128)S(1)}, f32[36,128]{1,0:T(8,128)S(1)}, u32[]{:S(2)}, u32[]{:S(2)}) collective-permute-start(f32[36,128]{1,0:T(8,128)S(1)} %add.23.refs_0_), channel_id=1, source_target_pairs={{0,20},{1,21},{2,22},{3,23},{4,16},{5,17},{6,18},{7,19},{8,28},{9,... | collective-permute-start | bytes 55304 | tf_op jit(solution)/shard_map/ppermute | solution.py:183
  24.7 5.3 %collective-permute-start.7 = (f32[36,128]{1,0:T(8,128)S(1)}, f32[36,128]{1,0:T(8,128)S(1)}, u32[]{:S(2)}, u32[]{:S(2)}) collective-permute-start(f32[36,128]{1,0:T(8,128)S(1)} %shard_map.86.refs_0_), channel_id=1, source_target_pairs={{0,7},{1,6},{2,5},{3,4},{4,3},{5,2},{6,1},{7,0},{8,15},{9,14},{10,... | collective-permute-start | bytes 55304 | tf_op jit(solution)/shard_map/ppermute | solution.py:183
  24.8 5.3 %collective-permute-start.6 = (f32[36,128]{1,0:T(8,128)S(1)}, f32[36,128]{1,0:T(8,128)S(1)}, u32[]{:S(2)}, u32[]{:S(2)}) collective-permute-start(f32[36,128]{1,0:T(8,128)S(1)} %shard_map.86.refs_0_), channel_id=1, source_target_pairs={{0,6},{1,7},{2,4},{3,5},{4,2},{5,3},{6,0},{7,1},{8,14},{9,15},{10,... | collective-permute-start | bytes 55304 | tf_op jit(solution)/shard_map/ppermute | solution.py:183
  25.8 4.4 %collective-permute-start.5 = (f32[36,128]{1,0:T(8,128)S(1)}, f32[36,128]{1,0:T(8,128)S(1)}, u32[]{:S(2)}, u32[]{:S(2)}) collective-permute-start(f32[36,128]{1,0:T(8,128)S(1)} %shard_map.86.refs_0_), channel_id=1, source_target_pairs={{0,5},{1,4},{2,7},{3,6},{4,1},{5,0},{6,3},{7,2},{8,13},{9,12},{10,... | collective-permute-start | bytes 55304 | tf_op jit(solution)/shard_map/ppermute | solution.py:183

commit v4 on v3

--- a/solution.py
+++ b/solution.py
@@ -35,6 +35,15 @@
     key_row = lax.broadcasted_iota(jnp.int32, (rows, wide), 0)
     query_col = lax.broadcasted_iota(jnp.int32, (rows, wide), 1) & (rows - 1)
     return key_row, key_row <= query_col
+
+
+def start_kernel(base_ref, lengths_ref, start_ref):
+    docs, rows = lengths_ref.shape[1], start_ref.shape[1]
+    upto = lax.broadcasted_iota(jnp.int32, (docs, docs), 1) <= lax.broadcasted_iota(jnp.int32, (docs, docs), 0)
+    ends = jnp.sum(jnp.where(upto, lengths_ref[...], 0), axis=1, keepdims=True)
+    base = base_ref[0]
+    position = base + lax.broadcasted_iota(jnp.int32, (docs, rows), 1)
+    start_ref[...] = jnp.max(jnp.where(ends <= position, ends, 0), axis=0, keepdims=True) - base
 
 
 def near_kernel(start_ref, q_ref, c_ref, k_ref, v_ref, s_ref, d_ref, sum_ref):
@@ -55,54 +64,68 @@
         sum_ref[g : g + 1, :] = jnp.sum(total, axis=0, keepdims=True)
 
 
-def far_kernel(reach, start_ref, k_ref, q_ref, c_ref, s_ref, d_ref, sum_ref, *refs):
-    *far_refs, bias_ref, p_ref, g_ref = refs
-    kp_refs, vp_refs = far_refs[::2], far_refs[1::2]
+def prob_kernel(reach, start_ref, q_ref, s_ref, *refs):
+    *kp_refs, p_ref, low_ref, pick_ref = refs
     rows = q_ref.shape[0]
     wide = 2 * rows
+    spill = spill_of(start_ref[...])
+    taken = lax.broadcasted_iota(jnp.int32, (2 * Q_HEADS, rows), 0)
+    taken = taken - jnp.where(lax.broadcasted_iota(jnp.int32, (2 * Q_HEADS, rows), 1) < spill, 0, Q_HEADS)
+    for h in range(Q_HEADS):
+        pick_ref[:, h * rows : (h + 1) * rows] = jnp.where(taken == h, 1.0, 0.0).astype(jnp.bfloat16)
     key_row, near = grids(rows, wide)
     start = jnp.concatenate([start_ref[...]] * 2, axis=1)
     far = jnp.logical_not(near) & (key_row - reach * rows >= start)
     valids = [key_row - j * rows >= start for j in range(1, reach)]
     order = [reach] + list(range(1, reach))
-    spill = spill_of(start_ref[...])
-    lane = lax.broadcasted_iota(jnp.int32, (rows, HEAD_DIM), 1)
-    row = lax.broadcasted_iota(jnp.int32, (rows, HEAD_DIM), 0)
-    spilled = row < spill
-    indicator = jnp.concatenate(
-        [jnp.where(lane == jnp.where(spilled, i, i + GROUP), 1.0, 0.0).astype(jnp.bfloat16) for i in range(GROUP)], axis=0)
-    far_sum = jnp.logical_not(spilled) & (lane < GROUP)
+    cut = [slice(i * rows, (i + 1) * rows) for i in range(reach)]
+    for pair in range(Q_HEADS // 2):
+        g, first = 2 * pair // GROUP, 2 * pair
+        at = slice(first * rows, (first + 2) * rows)
+        far_key = jnp.concatenate([head(kp_refs[j - 1], g) for j in order], axis=0)
+        q_two = jnp.concatenate([head(q_ref, first), head(q_ref, first + 1)], axis=0)
+        s_far = dot(far_key, q_two, NT)
+        s_parts = [jnp.where(far, s_far[cut[0]] * (SCALE * LOG2E), s_ref[:, at])]
+        s_parts += [jnp.where(ok, s_far[c] * (SCALE * LOG2E), -1e30) for ok, c in zip(valids, cut[1:])]
+        top = functools.reduce(jnp.maximum, [jnp.max(s, axis=0, keepdims=True) for s in s_parts])
+        e_parts = [jnp.exp2(s - top) for s in s_parts]
+        inv = 1.0 / sum(jnp.sum(e, axis=0, keepdims=True) for e in e_parts)
+        for e, c in zip(e_parts, cut):
+            prob = e * inv
+            p_ref[c, at] = prob
+            low_ref[c, at] = prob.astype(jnp.bfloat16)
+
+
+def far_kernel(reach, start_ref, k_ref, c_ref, d_ref, sum_ref, p_ref, pick_ref, *refs):
+    kp_refs, vp_refs = refs[:reach], refs[reach : 2 * reach]
+    bias_ref, g_ref = refs[2 * reach :]
+    rows = c_ref.shape[0]
+    _, near = grids(rows, 2 * rows)
+    order = [reach] + list(range(1, reach))
+    cut = [slice(i * rows, (i + 1) * rows) for i in range(reach)]
     bias_ref[Q_HEADS:, :] = sum_ref[:KV_HEADS]
     for g in range(KV_HEADS):
-        far_key = jnp.concatenate([head(kp_refs[j - 1], g) for j in order], axis=0)
         far_value = jnp.concatenate([head(vp_refs[j - 1], g) for j in order], axis=0)
         for pair in range(GROUP // 2):
             first = g * GROUP + 2 * pair
             at = slice(first * rows, (first + 2) * rows)
-            q_two = jnp.concatenate([head(q_ref, first), head(q_ref, first + 1)], axis=0)
             c_two = jnp.concatenate([head(c_ref, first), head(c_ref, first + 1)], axis=0)
-            s_far = dot(far_key, q_two, NT)
             d_far = dot(far_value, c_two, NT)
-            cut = [slice(i * rows, (i + 1) * rows) for i in range(reach)]
-            s_parts = [jnp.where(far, s_far[cut[0]] * (SCALE * LOG2E), s_ref[:, at])]
-            s_parts += [jnp.where(ok, s_far[c] * (SCALE * LOG2E), -1e30) for ok, c in zip(valids, cut[1:])]
             d_parts = [jnp.where(near, d_ref[:, at], d_far[cut[0]])] + [d_far[c] for c in cut[1:]]
-            top = functools.reduce(jnp.maximum, [jnp.max(s, axis=0, keepdims=True) for s in s_parts])
-            e_parts = [jnp.exp2(s - top) for s in s_parts]
-            total = sum(jnp.sum(e, axis=0, keepdims=True) for e in e_parts)
-            inv = 1.0 / total
-            delta = inv * sum(jnp.sum(e * d, axis=0, keepdims=True) for e, d in zip(e_parts, d_parts))
-            for e, d, c in zip(e_parts, d_parts, cut):
-                prob = e * inv
-                p_ref[c, at] = prob.astype(jnp.bfloat16)
-                g_ref[c, at] = (prob * (d - delta)).astype(jnp.bfloat16)
-        sums = dot(g_ref[:, g * GROUP * rows : (g + 1) * GROUP * rows], indicator, NN) * SCALE
-        own_sums = jnp.where(far_sum, 0.0, sums[:rows]).astype(jnp.bfloat16)
-        far_sums = jnp.where(far_sum, sums[:rows], 0.0).astype(jnp.bfloat16)
-        if reach > 1:
-            far_sums = jnp.concatenate([far_sums, sums[rows:].astype(jnp.bfloat16)], axis=0)
-        query_bias = dot(own_sums, head(k_ref, g), TN) + dot(far_sums, far_key, TN)
-        bias_ref[g * GROUP : (g + 1) * GROUP, :] = query_bias[:GROUP] + query_bias[GROUP : 2 * GROUP]
+            delta = sum(jnp.sum(p_ref[c, at] * d, axis=0, keepdims=True) for d, c in zip(d_parts, cut))
+            for d, c in zip(d_parts, cut):
+                g_ref[c, at] = (p_ref[c, at] * (d - delta)).astype(jnp.bfloat16)
+    total = dot(pick_ref[...], g_ref[...], NT) * SCALE
+    early, late = total[:Q_HEADS], total[Q_HEADS:]
+    spilled = lax.broadcasted_iota(jnp.int32, (Q_HEADS, rows), 1) < spill_of(start_ref[...])
+    own_sums = (late[:, :rows] + jnp.where(spilled, early[:, :rows], 0.0)).astype(jnp.bfloat16)
+    far_sums = [jnp.where(spilled, 0.0, early[:, :rows]).astype(jnp.bfloat16)]
+    far_sums += [(early + late)[:, c].astype(jnp.bfloat16) for c in cut[1:]]
+    query_bias = dot(own_sums, k_ref[...], NN)
+    for far_sum, j in zip(far_sums, order):
+        query_bias = query_bias + dot(far_sum, kp_refs[j - 1][...], NN)
+    for g in range(KV_HEADS):
+        bias_ref[g * GROUP : (g + 1) * GROUP, :] = query_bias[g * GROUP : (g + 1) * GROUP, g * HEAD_DIM : (g + 1) * HEAD_DIM]
 
 
 def grad_kernel(reach, start_ref, q_ref, c_ref, p_ref, g_ref, own_ref, *back_refs):
@@ -126,12 +149,12 @@
                 back_refs[j - 1][:, to] = (late + early)[i * rows : (i + 1) * rows].astype(jnp.bfloat16)
 
 
-def call(kernel, args, outs, flops, scratch=()):
+def call(kernel, args, outs, flops, scratch=(), scalars=0):
     vmem = pl.BlockSpec(memory_space=pltpu.VMEM)
     return pl.pallas_call(
         kernel,
         out_shape=[jax.ShapeDtypeStruct(*out) for out in outs],
-        in_specs=[vmem] * len(args),
+        in_specs=[pl.BlockSpec(memory_space=pltpu.SMEM)] * scalars + [vmem] * (len(args) - scalars),
         out_specs=[vmem] * len(outs),
         scratch_shapes=scratch,
         compiler_params=pltpu.CompilerParams(vmem_limit_bytes=32 * 1024 * 1024),
@@ -144,14 +167,22 @@
     kv_feat = keys.shape[1]
     unit = 2 * rows * rows * Q_HEADS * HEAD_DIM
     square = ((rows, Q_HEADS * rows), jnp.float32)
-    slots = ((reach * rows, Q_HEADS * rows), jnp.bfloat16)
+    slots = (reach * rows, Q_HEADS * rows)
     block = ((rows, 2 * kv_feat), jnp.bfloat16)
-    near = call(near_kernel, (start, query, cotangent, keys, values), [square, square, ((8, HEAD_DIM), jnp.float32)], 2 * unit)
-    bias, probs, grads = call(
+    near_s, near_d, sums = call(
+        near_kernel, (start, query, cotangent, keys, values), [square, square, ((8, HEAD_DIM), jnp.float32)], 2 * unit
+    )
+    wide_probs, probs, pick = call(
+        functools.partial(prob_kernel, reach),
+        (start, query, near_s, *far[::2]),
+        [(slots, jnp.float32), (slots, jnp.bfloat16), ((2 * Q_HEADS, Q_HEADS * rows), jnp.bfloat16)],
+        reach * unit,
+    )
+    bias, grads = call(
         functools.partial(far_kernel, reach),
-        (start, keys, query, cotangent, *near, *far),
-        [((Q_HEADS + KV_HEADS, HEAD_DIM), jnp.float32), slots, slots],
-        3 * reach * unit,
+        (start, keys, cotangent, near_d, sums, wide_probs, pick, *far[::2], *far[1::2]),
+        [((Q_HEADS + KV_HEADS, HEAD_DIM), jnp.float32), (slots, jnp.bfloat16)],
+        2 * reach * unit,
     )
 
     def gradients(start):
@@ -166,7 +197,8 @@
     return lax.ppermute(array, AXES, [(i, (i + by) % count) for i in range(count)])
 
 
-EXCHANGE_FLOPS = 2360_000_000
+START_FLOPS = 3000_000_000
+EXCHANGE_FLOPS = 2300_000_000
 
 
 def stages(count, ctx):
@@ -238,10 +270,8 @@
     reach = lax.axis_size("ctx") // 4
     device = lax.axis_index(AXES)
     far = [shift(x, count, distance) for distance in range(1, reach + 1) for x in (keys, values)]
-    ends = jnp.cumsum(doc_lengths)
-    position = device * rows + jnp.arange(rows, dtype=jnp.int32)
-    start = jnp.max(jnp.where(ends[:, None] <= position[None, :], ends[:, None], 0), axis=0)
-    start = (start - device * rows)[None, :]
+    base = (device * rows).reshape(1)
+    (start,) = call(start_kernel, (base, doc_lengths.reshape(1, -1)), [((1, rows), jnp.int32)], START_FLOPS, (), 1)
     bias, gradients = attend(reach, start, query, cotangent, keys, values, far)
     steps = stages(count, lax.axis_size("ctx"))
     parts = None

time: 31.2 us -> 29.7 us (0.952)
  local copies, waits for them, and re-layouts: 5 us -> 2.11 us
  waiting for transfers between devices: 7.28 us -> 8.57 us
  starting transfers between devices: 12.5 us -> 12.9 us
    unnamed x8 -> x10, local copies, waits for them, and re-layouts: 4.25 us -> 2.11 us
    ppermute x3, waiting for transfers between devices: 1.9 us -> 3.68 us  [shift(): lax.ppermute(array, AXES, [(i, (i + by) % count) for i in range(count)])]
    ppermute x6, starting transfers between devices: 5.57 us -> 6.36 us  [exchange(): lax.ppermute(array, AXES, [(i, i ^ mask) for i in range(count)])]
    another operation x1 -> x0, local copies, waits for them, and re-layouts: 0.74 us -> none
    ppermute x6, waiting for transfers between devices: 5.38 us -> 4.89 us  [exchange(): lax.ppermute(array, AXES, [(i, i ^ mask) for i in range(count)])]
    ppermute x3, starting transfers between devices: 6.9 us -> 6.51 us  [shift(): lax.ppermute(array, AXES, [(i, (i + by) % count) for i in range(count)])]
    pallas_call x4 -> x6, Pallas kernels: 4.41 us -> 4.48 us  [call(): pl.pallas_call(kernel, out_shape=[jax.ShapeDtypeStruct(*out) for out in o...]
  transfers between devices with their start and end apart: 9 -> 9, of which waited for: 5 -> 6; matrix products, arithmetic and copies ran while one was open for 3% -> 0% of each run, Pallas kernels for 6% -> 11%
where the time goes in v4:
time: 29.7 us; the launch traced here: 29.5 us
  starting transfers between devices  12.9 us (43%)
  waiting for transfers between devices  8.57 us (29%)
  Pallas kernels  5.25 us (18%)
  local copies, waits for them, and re-layouts  2.11 us (7%)
  between operations  0.7 us (2%)
    ppermute x3, starting transfers between devices, shift(): lax.ppermute(array, AXES, [(i, (i + by) % count) for i in range(count)])  6.51 us
    ppermute x6, starting transfers between devices, exchange(): lax.ppermute(array, AXES, [(i, i ^ mask) for i in range(count)])  6.36 us
    ppermute x6, waiting for transfers between devices, exchange(): lax.ppermute(array, AXES, [(i, i ^ mask) for i in range(count)])  4.89 us
    pallas_call x6, Pallas kernels, call(): pl.pallas_call(kernel, out_shape=[jax.ShapeDtypeStruct(*out) for out in o...  4.48 us
    ppermute x3, waiting for transfers between devices, shift(): lax.ppermute(array, AXES, [(i, (i + by) % count) for i in range(count)])  3.68 us
    unnamed x10, local copies, waits for them, and re-layouts  2.11 us
    pallas_call x1, Pallas kernels, last(): pl.pallas_call(functools.partial(last_kernel, len(terms), len(parts)), ou...  0.77 us
  transfers between devices with their start and end apart: 9, of which 6 were waited for; matrix products, arithmetic and copies ran while one was open for 0% of the time, Pallas kernels for 11%

profile of v4, /device:TPU:0, one launch (start us, length us, event | category | flops | bytes accessed | tf_op | source)
XLA Modules:
  0.0 29.5 jit_solution(18126304984676256709)
XLA Ops:
  0.6 3.1 %collective-permute-start = (bf16[128,512]{1,0:T(8,128)(2,1)}, bf16[128,512]{1,0:T(8,128)(2,1)S(1)}, u32[]{:S(2)}, u32[]{:S(2)}) collective-permute-start(bf16[128,512]{1,0:T(8,128)(2,1)} %k_ref.3), channel_id=1, source_target_pairs={{0,1},{1,2},{2,3},{3,4},{4,5},{5,6},{6,7},{7,8},{8,9},{9,10},{10,1... | collective-permute-start | bytes 393224 | tf_op jit(solution)/shard_map/ppermute | solution.py:197
  3.7 1.6 %collective-permute-start.1 = (bf16[128,512]{1,0:T(8,128)(2,1)}, bf16[128,512]{1,0:T(8,128)(2,1)S(1)}, u32[]{:S(2)}, u32[]{:S(2)}) collective-permute-start(bf16[128,512]{1,0:T(8,128)(2,1)} %v_ref.1), channel_id=1, source_target_pairs={{0,1},{1,2},{2,3},{3,4},{4,5},{5,6},{6,7},{7,8},{8,9},{9,10},{10,1... | collective-permute-start | bytes 393224 | tf_op jit(solution)/shard_map/ppermute | solution.py:197
  5.3 0.0 copy-start.4
  5.3 0.7 %copy-done.4 = s32[64]{0:T(128)S(1)} copy-done((s32[64]{0:T(128)S(1)}, s32[64]{0:T(128)}, u32[]{:S(2)}) %copy-start.4) | copy-done | bytes 280
  5.9 0.0 copy-start
  5.9 0.0 copy-start.1
  6.0 0.1 shard_map.84.start_ref
  6.1 1.1 %copy-done = bf16[128,4096]{1,0:T(8,128)(2,1)S(1)} copy-done((bf16[128,4096]{1,0:T(8,128)(2,1)S(1)}, bf16[128,4096]{1,0:T(8,128)(2,1)}, u32[]{:S(2)}) %copy-start) | copy-done | bytes 1048600
  7.2 0.3 %copy-done.1 = bf16[128,4096]{1,0:T(8,128)(2,1)S(1)} copy-done((bf16[128,4096]{1,0:T(8,128)(2,1)S(1)}, bf16[128,4096]{1,0:T(8,128)(2,1)}, u32[]{:S(2)}) %copy-start.1) | copy-done | bytes 1048600
  7.5 0.0 copy-done.2
  7.5 0.0 copy-done.3
  7.5 0.8 %shard_map.85 = (f32[128,4096]{1,0:T(8,128)S(1)}, f32[128,4096]{1,0:T(8,128)S(1)}, f32[8,128]{1,0:T(8,128)S(1)}) custom-call(s32[1,128]{1,0:T(1,128)S(1)} %shard_map.84.start_ref, bf16[128,4096]{1,0:T(8,128)(2,1)S(1)} %copy-done.1, bf16[128,4096]{1,0:T(8,128)(2,1)S(1)} %copy-done, bf16[128,512]{1,0:T(8,128)(2,1)S(1)} %copy-done.2, bf16[128,512]{1,0:T(8,128)(2,1)S(1)} %copy-done.3), custom_call_target="tpu_custom_call" | custom-call | flops 268435456 | bytes 2097152 | tf_op jit(solution)/shard_map/pallas_call | solution.py:154
  8.3 2.2 %collective-permute-done.refs_0_ = bf16[128,512]{1,0:T(8,128)(2,1)S(1)} collective-permute-done((bf16[128,512]{1,0:T(8,128)(2,1)}, bf16[128,512]{1,0:T(8,128)(2,1)S(1)}, u32[]{:S(2)}, u32[]{:S(2)}) %collective-permute-start) | collective-permute-done | bytes 131104 | tf_op jit(solution)/shard_map/ppermute | solution.py:197
  10.5 1.3 %shard_map.86 = (f32[128,4096]{1,0:T(8,128)S(1)}, bf16[128,4096]{1,0:T(8,128)(2,1)S(1)}, bf16[64,4096]{1,0:T(8,128)(2,1)S(1)}) custom-call(s32[1,128]{1,0:T(1,128)S(1)} %shard_map.84.start_ref, bf16[128,4096]{1,0:T(8,128)(2,1)S(1)} %copy-done.1, f32[128,4096]{1,0:T(8,128)S(1)} %get-tuple-element.22.s_ref, bf16[128,512]{1,0:T(8,128)(2,1)S(1)} %collective-permute-done.refs_0_), custom_call_target="tpu_custom_call" | custom-call | flops 134217728 | bytes 2097152 | tf_op jit(solution)/shard_map/pallas_call | solution.py:154
  11.8 1.5 %collective-permute-done.1.refs_1_ = bf16[128,512]{1,0:T(8,128)(2,1)S(1)} collective-permute-done((bf16[128,512]{1,0:T(8,128)(2,1)}, bf16[128,512]{1,0:T(8,128)(2,1)S(1)}, u32[]{:S(2)}, u32[]{:S(2)}) %collective-permute-start.1) | collective-permute-done | bytes 131104 | tf_op jit(solution)/shard_map/ppermute | solution.py:197
  13.3 1.3 %shard_map.87 = (f32[36,128]{1,0:T(8,128)S(1)}, bf16[128,4096]{1,0:T(8,128)(2,1)S(1)}) custom-call(s32[1,128]{1,0:T(1,128)S(1)} %shard_map.84.start_ref, bf16[128,512]{1,0:T(8,128)(2,1)S(1)} %copy-done.2, bf16[128,4096]{1,0:T(8,128)(2,1)S(1)} %copy-done, f32[128,4096]{1,0:T(8,128)S(1)} %get-tuple-element.20.d_ref, f32[8,128]{1,0:T(8,128)S(1)} %get-tuple-element.21.sum_ref, ...), custom_call_target="tpu_custom_call" | custom-call | flops 268435456 | bytes 2097152 | tf_op jit(solution)/shard_map/pallas_call | solution.py:154
  14.7 0.1 collective-permute-start.2
  14.8 1.2 %collective-permute-done.2 = f32[36,128]{1,0:T(8,128)S(1)} collective-permute-done((f32[36,128]{1,0:T(8,128)S(1)}, f32[36,128]{1,0:T(8,128)S(1)}, u32[]{:S(2)}, u32[]{:S(2)}) %collective-permute-start.2) | collective-permute-done | bytes 18464 | tf_op jit(solution)/shard_map/ppermute | solution.py:215
  15.9 1.0 %collective-permute-start.3 = (f32[36,128]{1,0:T(8,128)S(1)}, f32[36,128]{1,0:T(8,128)S(1)}, u32[]{:S(2)}, u32[]{:S(2)}) collective-permute-start(f32[36,128]{1,0:T(8,128)S(1)} %add.10), channel_id=1, source_target_pairs={{0,12},{1,13},{2,14},{3,15},{4,8},{5,9},{6,10},{7,11},{8,4},{9,5},... | collective-permute-start | bytes 55304 | tf_op jit(solution)/shard_map/ppermute | solution.py:215
  17.0 0.9 %shard_map.89 = (bf16[128,1024]{1,0:T(8,128)(2,1)S(1)}, bf16[128,1024]{1,0:T(8,128)(2,1)S(1)}) custom-call(s32[1,128]{1,0:T(1,128)S(1)} %shard_map.84.start_ref, bf16[128,4096]{1,0:T(8,128)(2,1)S(1)} %copy-done.1, bf16[128,4096]{1,0:T(8,128)(2,1)S(1)} %copy-done, bf16[128,4096]{1,0:T(8,128)(2,1)S(1)} %get-tuple-element.28.p_ref, ...), custom_call_target="tpu_custom_call" | custom-call | flops 268435456 | bytes 2097152 | tf_op jit(solution)/shard_map/pallas_call | solution.py:154
  17.9 1.9 %collective-permute-start.8 = (bf16[128,1024]{1,0:T(8,128)(2,1)S(1)}, bf16[128,1024]{1,0:T(8,128)(2,1)S(1)}, u32[]{:S(2)}, u32[]{:S(2)}) collective-permute-start(bf16[128,1024]{1,0:T(8,128)(2,1)S(1)} %get-tuple-element.31), channel_id=1, source_target_pairs={{0,31},{1,0},{2,1},{3,2},{4,3},{5,4},{6,5},{7,6},{8,7},{9,8},{10,9... | collective-permute-start | bytes 786440 | tf_op jit(solution)/shard_map/ppermute | solution.py:197
  19.7 0.0 collective-permute-done.3
  19.7 1.4 %collective-permute-start.4 = (f32[36,128]{1,0:T(8,128)S(1)}, f32[36,128]{1,0:T(8,128)S(1)}, u32[]{:S(2)}, u32[]{:S(2)}) collective-permute-start(f32[36,128]{1,0:T(8,128)S(1)} %add.11.refs_0_), channel_id=1, source_target_pairs={{0,20},{1,21},{2,22},{3,23},{4,16},{5,17},{6,18},{7,19},{8,28},{9,... | collective-permute-start | bytes 55304 | tf_op jit(solution)/shard_map/ppermute | solution.py:215
  21.1 2.0 %collective-permute-done.4.refs_1_ = f32[36,128]{1,0:T(8,128)S(1)} collective-permute-done((f32[36,128]{1,0:T(8,128)S(1)}, f32[36,128]{1,0:T(8,128)S(1)}, u32[]{:S(2)}, u32[]{:S(2)}) %collective-permute-start.4) | collective-permute-done | bytes 18464 | tf_op jit(solution)/shard_map/ppermute | solution.py:215
  23.1 0.1 collective-permute-start.5
  23.2 0.1 collective-permute-start.6
  23.3 3.7 %collective-permute-start.7 = (f32[36,128]{1,0:T(8,128)S(1)}, f32[36,128]{1,0:T(8,128)S(1)}, u32[]{:S(2)}, u32[]{:S(2)}) collective-permute-start(f32[36,128]{1,0:T(8,128)S(1)} %shard_map.88.refs_0_), channel_id=1, source_target_pairs={{0,7},{1,6},{2,5},{3,4},{4,3},{5,2},{6,1},{7,0},{8,15},{9,14},{10,... | collective-permute-start | bytes 55304 | tf_op jit(solution)/shard_map/ppermute | solution.py:215
  27.1 0.0 collective-permute-done.5.refs_1_
  27.1 0.3 collective-permute-done.6.refs_2_
  27.3 1.4 %collective-permute-done.7.refs_3_ = f32[36,128]{1,0:T(8,128)S(1)} collective-permute-done((f32[36,128]{1,0:T(8,128)S(1)}, f32[36,128]{1,0:T(8,128)S(1)}, u32[]{:S(2)}, u32[]{:S(2)}) %collective-permute-start.7) | collective-permute-done | bytes 18464 | tf_op jit(solution)/shard_map/ppermute | solution.py:215
  28.7 0.0 collective-permute-done.8.refs_5_
  28.7 0.8 %shard_map.90 = (f32[32,128]{1,0:T(8,128)}, f32[4,128]{1,0:T(4,128)}, bf16[128,512]{1,0:T(8,128)(2,1)}, bf16[128,512]{1,0:T(8,128)(2,1)}) custom-call(f32[36,128]{1,0:T(8,128)S(1)} %shard_map.88.refs_0_, f32[36,128]{1,0:T(8,128)S(1)} %collective-permute-done.5.refs_1_, f32[36,128]{1,0:T(8,128)S(1)} %collective-permute-done.6.refs_2_, ...), custom_call_target="tpu_custom_call" | custom-call | tf_op jit(solution)/shard_map/pallas_call | solution.py:256
  (5 shorter events, 0.0 us)
Async XLA Ops:
  0.6 9.9 %collective-permute-start = (bf16[128,512]{1,0:T(8,128)(2,1)}, bf16[128,512]{1,0:T(8,128)(2,1)S(1)}, u32[]{:S(2)}, u32[]{:S(2)}) collective-permute-start(bf16[128,512]{1,0:T(8,128)(2,1)} %k_ref.3), channel_id=1, source_target_pairs={{0,1},{1,2},{2,3},{3,4},{4,5},{5,6},{6,7},{7,8},{8,9},{9,10},{10,1... | collective-permute-start | bytes 393224 | tf_op jit(solution)/shard_map/ppermute | solution.py:197
  3.7 9.6 %collective-permute-start.1 = (bf16[128,512]{1,0:T(8,128)(2,1)}, bf16[128,512]{1,0:T(8,128)(2,1)S(1)}, u32[]{:S(2)}, u32[]{:S(2)}) collective-permute-start(bf16[128,512]{1,0:T(8,128)(2,1)} %v_ref.1), channel_id=1, source_target_pairs={{0,1},{1,2},{2,3},{3,4},{4,5},{5,6},{6,7},{7,8},{8,9},{9,10},{10,1... | collective-permute-start | bytes 393224 | tf_op jit(solution)/shard_map/ppermute | solution.py:197
  5.3 0.7 %copy-start.4 = (s32[64]{0:T(128)S(1)}, s32[64]{0:T(128)}, u32[]{:S(2)}) copy-start(s32[64]{0:T(128)} %param.9) | copy-start | bytes 772
  5.9 1.2 %copy-start = (bf16[128,4096]{1,0:T(8,128)(2,1)S(1)}, bf16[128,4096]{1,0:T(8,128)(2,1)}, u32[]{:S(2)}) copy-start(bf16[128,4096]{1,0:T(8,128)(2,1)} %c_ref.5) | copy-start | bytes 3145732
  5.9 1.5 %copy-start.1 = (bf16[128,4096]{1,0:T(8,128)(2,1)S(1)}, bf16[128,4096]{1,0:T(8,128)(2,1)}, u32[]{:S(2)}) copy-start(bf16[128,4096]{1,0:T(8,128)(2,1)} %q_ref.5) | copy-start | bytes 3145732
  5.9 1.5 %copy-start.2 = (bf16[128,512]{1,0:T(8,128)(2,1)S(1)}, bf16[128,512]{1,0:T(8,128)(2,1)}, u32[]{:S(2)}) copy-start(bf16[128,512]{1,0:T(8,128)(2,1)} %k_ref.3) | copy-start | bytes 393220
  6.0 1.6 %copy-start.3 = (bf16[128,512]{1,0:T(8,128)(2,1)S(1)}, bf16[128,512]{1,0:T(8,128)(2,1)}, u32[]{:S(2)}) copy-start(bf16[128,512]{1,0:T(8,128)(2,1)} %v_ref.1) | copy-start | bytes 393220
  14.7 1.3 %collective-permute-start.2 = (f32[36,128]{1,0:T(8,128)S(1)}, f32[36,128]{1,0:T(8,128)S(1)}, u32[]{:S(2)}, u32[]{:S(2)}) collective-permute-start(f32[36,128]{1,0:T(8,128)S(1)} %get-tuple-element.25), channel_id=1, source_target_pairs={{0,4},{1,5},{2,6},{3,7},{4,0},{5,1},{6,2},{7,3},{8,12},{9,13},{10,... | collective-permute-start | bytes 55304 | tf_op jit(solution)/shard_map/ppermute | solution.py:215
  15.9 3.8 %collective-permute-start.3 = (f32[36,128]{1,0:T(8,128)S(1)}, f32[36,128]{1,0:T(8,128)S(1)}, u32[]{:S(2)}, u32[]{:S(2)}) collective-permute-start(f32[36,128]{1,0:T(8,128)S(1)} %add.10), channel_id=1, source_target_pairs={{0,12},{1,13},{2,14},{3,15},{4,8},{5,9},{6,10},{7,11},{8,4},{9,5},... | collective-permute-start | bytes 55304 | tf_op jit(solution)/shard_map/ppermute | solution.py:215
  17.9 10.9 %collective-permute-start.8 = (bf16[128,1024]{1,0:T(8,128)(2,1)S(1)}, bf16[128,1024]{1,0:T(8,128)(2,1)S(1)}, u32[]{:S(2)}, u32[]{:S(2)}) collective-permute-start(bf16[128,1024]{1,0:T(8,128)(2,1)S(1)} %get-tuple-element.31), channel_id=1, source_target_pairs={{0,31},{1,0},{2,1},{3,2},{4,3},{5,4},{6,5},{7,6},{8,7},{9,8},{10,9... | collective-permute-start | bytes 786440 | tf_op jit(solution)/shard_map/ppermute | solution.py:197
  19.7 3.4 %collective-permute-start.4 = (f32[36,128]{1,0:T(8,128)S(1)}, f32[36,128]{1,0:T(8,128)S(1)}, u32[]{:S(2)}, u32[]{:S(2)}) collective-permute-start(f32[36,128]{1,0:T(8,128)S(1)} %add.11.refs_0_), channel_id=1, source_target_pairs={{0,20},{1,21},{2,22},{3,23},{4,16},{5,17},{6,18},{7,19},{8,28},{9,... | collective-permute-start | bytes 55304 | tf_op jit(solution)/shard_map/ppermute | solution.py:215
  23.1 3.9 %collective-permute-start.5 = (f32[36,128]{1,0:T(8,128)S(1)}, f32[36,128]{1,0:T(8,128)S(1)}, u32[]{:S(2)}, u32[]{:S(2)}) collective-permute-start(f32[36,128]{1,0:T(8,128)S(1)} %shard_map.88.refs_0_), channel_id=1, source_target_pairs={{0,5},{1,4},{2,7},{3,6},{4,1},{5,0},{6,3},{7,2},{8,13},{9,12},{10,... | collective-permute-start | bytes 55304 | tf_op jit(solution)/shard_map/ppermute | solution.py:215
  23.2 4.1 %collective-permute-start.6 = (f32[36,128]{1,0:T(8,128)S(1)}, f32[36,128]{1,0:T(8,128)S(1)}, u32[]{:S(2)}, u32[]{:S(2)}) collective-permute-start(f32[36,128]{1,0:T(8,128)S(1)} %shard_map.88.refs_0_), channel_id=1, source_target_pairs={{0,6},{1,7},{2,4},{3,5},{4,2},{5,3},{6,0},{7,1},{8,14},{9,15},{10,... | collective-permute-start | bytes 55304 | tf_op jit(solution)/shard_map/ppermute | solution.py:215
  23.3 5.4 %collective-permute-start.7 = (f32[36,128]{1,0:T(8,128)S(1)}, f32[36,128]{1,0:T(8,128)S(1)}, u32[]{:S(2)}, u32[]{:S(2)}) collective-permute-start(f32[36,128]{1,0:T(8,128)S(1)} %shard_map.88.refs_0_), channel_id=1, source_target_pairs={{0,7},{1,6},{2,5},{3,4},{4,3},{5,2},{6,1},{7,0},{8,15},{9,14},{10,... | collective-permute-start | bytes 55304 | tf_op jit(solution)/shard_map/ppermute | solution.py:215

commit v5 on v4

--- a/solution.py
+++ b/solution.py
@@ -203,8 +203,9 @@
 
 def stages(count, ctx):
     powers = [1 << i for i in range(count.bit_length() - 1)]
-    masks = [[ctx]] + [[p ^ ctx] for p in powers if p > ctx]
+    outer = [p for p in powers if p > ctx]
     inner = [p for p in powers if p < ctx]
+    masks = [[ctx, outer[0] ^ ctx, outer[0]]] + [[p ^ ctx] for p in outer[1:]]
     for i in range(0, len(inner), 2):
         pair = inner[i : i + 2]
         masks.append([p ^ ctx for p in pair] + ([pair[0] ^ pair[1] ^ ctx] if len(pair) > 1 else []))
@@ -274,14 +275,11 @@
     (start,) = call(start_kernel, (base, doc_lengths.reshape(1, -1)), [((1, rows), jnp.int32)], START_FLOPS, (), 1)
     bias, gradients = attend(reach, start, query, cotangent, keys, values, far)
     steps = stages(count, lax.axis_size("ctx"))
-    parts = None
+    own, *backs = gradients(start)
+    parts = [own] + [shift(backs[distance - 1], count, -distance) for distance in range(1, reach + 1)]
     for i, masks in enumerate(steps):
-        if i == 1:
-            start, bias = lax.optimization_barrier((start, bias))
-            own, *backs = gradients(start)
-            parts = [own] + [shift(backs[distance - 1], count, -distance) for distance in range(1, reach + 1)]
         terms = exchange(bias, masks, count)
-        bias = add(terms) if i == 2 else total_of(terms)
+        bias = add(terms) if i == 1 else total_of(terms)
     query_bias, value_bias, key_grad, value_grad = last(terms, parts)
     return (key_grad, value_grad, query_bias.reshape(-1), value_bias.reshape(-1))
 

time: 29.7 us -> 29.4 us (0.990)
  starting transfers between devices: 12.9 us -> 12.4 us
    ppermute x6 -> x7, starting transfers between devices: 6.36 us -> 5.52 us  [exchange(): lax.ppermute(array, AXES, [(i, i ^ mask) for i in range(count)])]
    ppermute x3, starting transfers between devices: 6.51 us -> 6.87 us  [shift(): lax.ppermute(array, AXES, [(i, (i + by) % count) for i in range(count)])]
    ppermute x6 -> x7, waiting for transfers between devices: 4.89 us -> 5.04 us  [exchange(): lax.ppermute(array, AXES, [(i, i ^ mask) for i in range(count)])]
  transfers between devices with their start and end apart: 9 -> 10, of which waited for: 6 -> 5; matrix products, arithmetic and copies ran while one was open for 0% -> 0% of each run, Pallas kernels for 11% -> 11%
where the time goes in v5:
time: 29.4 us; the launch traced here: 29.2 us
  starting transfers between devices  12.4 us (42%)
  waiting for transfers between devices  8.72 us (30%)
  Pallas kernels  5.25 us (18%)
  local copies, waits for them, and re-layouts  2.11 us (7%)
  between operations  0.7 us (2%)
    ppermute x3, starting transfers between devices, shift(): lax.ppermute(array, AXES, [(i, (i + by) % count) for i in range(count)])  6.87 us
    ppermute x7, starting transfers between devices, exchange(): lax.ppermute(array, AXES, [(i, i ^ mask) for i in range(count)])  5.52 us
    ppermute x7, waiting for transfers between devices, exchange(): lax.ppermute(array, AXES, [(i, i ^ mask) for i in range(count)])  5.04 us
    pallas_call x6, Pallas kernels, call(): pl.pallas_call(kernel, out_shape=[jax.ShapeDtypeStruct(*out) for out in o...  4.48 us
    ppermute x3, waiting for transfers between devices, shift(): lax.ppermute(array, AXES, [(i, (i + by) % count) for i in range(count)])  3.68 us
    unnamed x10, local copies, waits for them, and re-layouts  2.11 us
    pallas_call x1, Pallas kernels, last(): pl.pallas_call(functools.partial(last_kernel, len(terms), len(parts)), ou...  0.77 us
  transfers between devices with their start and end apart: 10, of which 5 were waited for; matrix products, arithmetic and copies ran while one was open for 0% of the time, Pallas kernels for 11%

profile of v5, /device:TPU:0, one launch (start us, length us, event | category | flops | bytes accessed | tf_op | source)
XLA Modules:
  0.0 29.2 jit_solution(11379614296428517865)
XLA Ops:
  0.6 3.1 %collective-permute-start = (bf16[128,512]{1,0:T(8,128)(2,1)}, bf16[128,512]{1,0:T(8,128)(2,1)S(1)}, u32[]{:S(2)}, u32[]{:S(2)}) collective-permute-start(bf16[128,512]{1,0:T(8,128)(2,1)} %k_ref.3), channel_id=1, source_target_pairs={{0,1},{1,2},{2,3},{3,4},{4,5},{5,6},{6,7},{7,8},{8,9},{9,10},{10,1... | collective-permute-start | bytes 393224 | tf_op jit(solution)/shard_map/ppermute | solution.py:197
  3.7 1.6 %collective-permute-start.1 = (bf16[128,512]{1,0:T(8,128)(2,1)}, bf16[128,512]{1,0:T(8,128)(2,1)S(1)}, u32[]{:S(2)}, u32[]{:S(2)}) collective-permute-start(bf16[128,512]{1,0:T(8,128)(2,1)} %v_ref.1), channel_id=1, source_target_pairs={{0,1},{1,2},{2,3},{3,4},{4,5},{5,6},{6,7},{7,8},{8,9},{9,10},{10,1... | collective-permute-start | bytes 393224 | tf_op jit(solution)/shard_map/ppermute | solution.py:197
  5.3 0.0 copy-start.4
  5.3 0.7 %copy-done.4 = s32[64]{0:T(128)S(1)} copy-done((s32[64]{0:T(128)S(1)}, s32[64]{0:T(128)}, u32[]{:S(2)}) %copy-start.4) | copy-done | bytes 280
  6.0 0.1 shard_map.84.start_ref
  6.1 1.1 %copy-done = bf16[128,4096]{1,0:T(8,128)(2,1)S(1)} copy-done((bf16[128,4096]{1,0:T(8,128)(2,1)S(1)}, bf16[128,4096]{1,0:T(8,128)(2,1)}, u32[]{:S(2)}) %copy-start) | copy-done | bytes 1048600
  7.2 0.3 %copy-done.1 = bf16[128,4096]{1,0:T(8,128)(2,1)S(1)} copy-done((bf16[128,4096]{1,0:T(8,128)(2,1)S(1)}, bf16[128,4096]{1,0:T(8,128)(2,1)}, u32[]{:S(2)}) %copy-start.1) | copy-done | bytes 1048600
  7.5 0.0 copy-done.2
  7.5 0.0 copy-done.3
  7.5 0.8 %shard_map.85 = (f32[128,4096]{1,0:T(8,128)S(1)}, f32[128,4096]{1,0:T(8,128)S(1)}, f32[8,128]{1,0:T(8,128)S(1)}) custom-call(s32[1,128]{1,0:T(1,128)S(1)} %shard_map.84.start_ref, bf16[128,4096]{1,0:T(8,128)(2,1)S(1)} %copy-done.1, bf16[128,4096]{1,0:T(8,128)(2,1)S(1)} %copy-done, bf16[128,512]{1,0:T(8,128)(2,1)S(1)} %copy-done.2, bf16[128,512]{1,0:T(8,128)(2,1)S(1)} %copy-done.3), custom_call_target="tpu_custom_call" | custom-call | flops 268435456 | bytes 2097152 | tf_op jit(solution)/shard_map/pallas_call | solution.py:154
  8.3 2.2 %collective-permute-done.refs_0_ = bf16[128,512]{1,0:T(8,128)(2,1)S(1)} collective-permute-done((bf16[128,512]{1,0:T(8,128)(2,1)}, bf16[128,512]{1,0:T(8,128)(2,1)S(1)}, u32[]{:S(2)}, u32[]{:S(2)}) %collective-permute-start) | collective-permute-done | bytes 131104 | tf_op jit(solution)/shard_map/ppermute | solution.py:197
  10.5 1.3 %shard_map.86 = (f32[128,4096]{1,0:T(8,128)S(1)}, bf16[128,4096]{1,0:T(8,128)(2,1)S(1)}, bf16[64,4096]{1,0:T(8,128)(2,1)S(1)}) custom-call(s32[1,128]{1,0:T(1,128)S(1)} %shard_map.84.start_ref, bf16[128,4096]{1,0:T(8,128)(2,1)S(1)} %copy-done.1, f32[128,4096]{1,0:T(8,128)S(1)} %get-tuple-element.20.s_ref, bf16[128,512]{1,0:T(8,128)(2,1)S(1)} %collective-permute-done.refs_0_), custom_call_target="tpu_custom_call" | custom-call | flops 134217728 | bytes 2097152 | tf_op jit(solution)/shard_map/pallas_call | solution.py:154
  11.8 1.5 %collective-permute-done.1.refs_1_ = bf16[128,512]{1,0:T(8,128)(2,1)S(1)} collective-permute-done((bf16[128,512]{1,0:T(8,128)(2,1)}, bf16[128,512]{1,0:T(8,128)(2,1)S(1)}, u32[]{:S(2)}, u32[]{:S(2)}) %collective-permute-start.1) | collective-permute-done | bytes 131104 | tf_op jit(solution)/shard_map/ppermute | solution.py:197
  13.3 1.3 %shard_map.87 = (f32[36,128]{1,0:T(8,128)S(1)}, bf16[128,4096]{1,0:T(8,128)(2,1)S(1)}) custom-call(s32[1,128]{1,0:T(1,128)S(1)} %shard_map.84.start_ref, bf16[128,512]{1,0:T(8,128)(2,1)S(1)} %copy-done.2, bf16[128,4096]{1,0:T(8,128)(2,1)S(1)} %copy-done, f32[128,4096]{1,0:T(8,128)S(1)} %get-tuple-element.18.d_ref, f32[8,128]{1,0:T(8,128)S(1)} %get-tuple-element.19.sum_ref, ...), custom_call_target="tpu_custom_call" | custom-call | flops 268435456 | bytes 2097152 | tf_op jit(solution)/shard_map/pallas_call | solution.py:154
  14.7 0.5 %collective-permute-start.3 = (f32[36,128]{1,0:T(8,128)S(1)}, f32[36,128]{1,0:T(8,128)S(1)}, u32[]{:S(2)}, u32[]{:S(2)}) collective-permute-start(f32[36,128]{1,0:T(8,128)S(1)} %get-tuple-element.23), channel_id=1, source_target_pairs={{0,12},{1,13},{2,14},{3,15},{4,8},{5,9},{6,10},{7,11},{8,4},{9,5},... | collective-permute-start | bytes 55304 | tf_op jit(solution)/shard_map/ppermute | solution.py:216
  15.2 0.8 %collective-permute-start.4 = (f32[36,128]{1,0:T(8,128)S(1)}, f32[36,128]{1,0:T(8,128)S(1)}, u32[]{:S(2)}, u32[]{:S(2)}) collective-permute-start(f32[36,128]{1,0:T(8,128)S(1)} %get-tuple-element.23), channel_id=1, source_target_pairs={{0,8},{1,9},{2,10},{3,11},{4,12},{5,13},{6,14},{7,15},{8,0},{9,1},... | collective-permute-start | bytes 55304 | tf_op jit(solution)/shard_map/ppermute | solution.py:216
  16.1 0.5 %collective-permute-start.2 = (f32[36,128]{1,0:T(8,128)S(1)}, f32[36,128]{1,0:T(8,128)S(1)}, u32[]{:S(2)}, u32[]{:S(2)}) collective-permute-start(f32[36,128]{1,0:T(8,128)S(1)} %get-tuple-element.23), channel_id=1, source_target_pairs={{0,4},{1,5},{2,6},{3,7},{4,0},{5,1},{6,2},{7,3},{8,12},{9,13},{10,... | collective-permute-start | bytes 55304 | tf_op jit(solution)/shard_map/ppermute | solution.py:216
  16.6 0.9 %shard_map.89 = (bf16[128,1024]{1,0:T(8,128)(2,1)S(1)}, bf16[128,1024]{1,0:T(8,128)(2,1)S(1)}) custom-call(s32[1,128]{1,0:T(1,128)S(1)} %shard_map.84.start_ref, bf16[128,4096]{1,0:T(8,128)(2,1)S(1)} %copy-done.1, bf16[128,4096]{1,0:T(8,128)(2,1)S(1)} %copy-done, bf16[128,4096]{1,0:T(8,128)(2,1)S(1)} %get-tuple-element.24.p_ref, ...), custom_call_target="tpu_custom_call" | custom-call | flops 268435456 | bytes 2097152 | tf_op jit(solution)/shard_map/pallas_call | solution.py:154
  17.5 2.2 %collective-permute-start.9 = (bf16[128,1024]{1,0:T(8,128)(2,1)S(1)}, bf16[128,1024]{1,0:T(8,128)(2,1)S(1)}, u32[]{:S(2)}, u32[]{:S(2)}) collective-permute-start(bf16[128,1024]{1,0:T(8,128)(2,1)S(1)} %get-tuple-element.27), channel_id=1, source_target_pairs={{0,31},{1,0},{2,1},{3,2},{4,3},{5,4},{6,5},{7,6},{8,7},{9,8},{10,9... | collective-permute-start | bytes 786440 | tf_op jit(solution)/shard_map/ppermute | solution.py:197
  19.7 0.0 collective-permute-done.3
  19.7 0.0 collective-permute-done.4
  19.7 0.0 collective-permute-done.2
  19.8 0.2 collective-permute-start.5
  19.9 3.1 %collective-permute-done.5.refs_1_ = f32[36,128]{1,0:T(8,128)S(1)} collective-permute-done((f32[36,128]{1,0:T(8,128)S(1)}, f32[36,128]{1,0:T(8,128)S(1)}, u32[]{:S(2)}, u32[]{:S(2)}) %collective-permute-start.5) | collective-permute-done | bytes 18464 | tf_op jit(solution)/shard_map/ppermute | solution.py:216
  23.0 0.3 %collective-permute-start.6 = (f32[36,128]{1,0:T(8,128)S(1)}, f32[36,128]{1,0:T(8,128)S(1)}, u32[]{:S(2)}, u32[]{:S(2)}) collective-permute-start(f32[36,128]{1,0:T(8,128)S(1)} %shard_map.88.refs_0_), channel_id=1, source_target_pairs={{0,5},{1,4},{2,7},{3,6},{4,1},{5,0},{6,3},{7,2},{8,13},{9,12},{10,... | collective-permute-start | bytes 55304 | tf_op jit(solution)/shard_map/ppermute | solution.py:216
  23.4 0.0 collective-permute-start.7
  23.4 3.1 %collective-permute-start.8 = (f32[36,128]{1,0:T(8,128)S(1)}, f32[36,128]{1,0:T(8,128)S(1)}, u32[]{:S(2)}, u32[]{:S(2)}) collective-permute-start(f32[36,128]{1,0:T(8,128)S(1)} %shard_map.88.refs_0_), channel_id=1, source_target_pairs={{0,7},{1,6},{2,5},{3,4},{4,3},{5,2},{6,1},{7,0},{8,15},{9,14},{10,... | collective-permute-start | bytes 55304 | tf_op jit(solution)/shard_map/ppermute | solution.py:216
  26.5 0.0 collective-permute-done.6.refs_1_
  26.5 1.1 %collective-permute-done.7.refs_2_ = f32[36,128]{1,0:T(8,128)S(1)} collective-permute-done((f32[36,128]{1,0:T(8,128)S(1)}, f32[36,128]{1,0:T(8,128)S(1)}, u32[]{:S(2)}, u32[]{:S(2)}) %collective-permute-start.7) | collective-permute-done | bytes 18464 | tf_op jit(solution)/shard_map/ppermute | solution.py:216
  27.5 0.9 %collective-permute-done.8.refs_3_ = f32[36,128]{1,0:T(8,128)S(1)} collective-permute-done((f32[36,128]{1,0:T(8,128)S(1)}, f32[36,128]{1,0:T(8,128)S(1)}, u32[]{:S(2)}, u32[]{:S(2)}) %collective-permute-start.8) | collective-permute-done | bytes 18464 | tf_op jit(solution)/shard_map/ppermute | solution.py:216
  28.4 0.0 collective-permute-done.9.refs_5_
  28.4 0.8 %shard_map.90 = (f32[32,128]{1,0:T(8,128)}, f32[4,128]{1,0:T(4,128)}, bf16[128,512]{1,0:T(8,128)(2,1)}, bf16[128,512]{1,0:T(8,128)(2,1)}) custom-call(f32[36,128]{1,0:T(8,128)S(1)} %shard_map.88.refs_0_, f32[36,128]{1,0:T(8,128)S(1)} %collective-permute-done.6.refs_1_, f32[36,128]{1,0:T(8,128)S(1)} %collective-permute-done.7.refs_2_, ...), custom_call_target="tpu_custom_call" | custom-call | tf_op jit(solution)/shard_map/pallas_call | solution.py:257
  (6 shorter events, 0.0 us)
Async XLA Ops:
  0.6 9.9 %collective-permute-start = (bf16[128,512]{1,0:T(8,128)(2,1)}, bf16[128,512]{1,0:T(8,128)(2,1)S(1)}, u32[]{:S(2)}, u32[]{:S(2)}) collective-permute-start(bf16[128,512]{1,0:T(8,128)(2,1)} %k_ref.3), channel_id=1, source_target_pairs={{0,1},{1,2},{2,3},{3,4},{4,5},{5,6},{6,7},{7,8},{8,9},{9,10},{10,1... | collective-permute-start | bytes 393224 | tf_op jit(solution)/shard_map/ppermute | solution.py:197
  3.7 9.6 %collective-permute-start.1 = (bf16[128,512]{1,0:T(8,128)(2,1)}, bf16[128,512]{1,0:T(8,128)(2,1)S(1)}, u32[]{:S(2)}, u32[]{:S(2)}) collective-permute-start(bf16[128,512]{1,0:T(8,128)(2,1)} %v_ref.1), channel_id=1, source_target_pairs={{0,1},{1,2},{2,3},{3,4},{4,5},{5,6},{6,7},{7,8},{8,9},{9,10},{10,1... | collective-permute-start | bytes 393224 | tf_op jit(solution)/shard_map/ppermute | solution.py:197
  5.3 0.7 %copy-start.4 = (s32[64]{0:T(128)S(1)}, s32[64]{0:T(128)}, u32[]{:S(2)}) copy-start(s32[64]{0:T(128)} %param.9) | copy-start | bytes 772
  5.9 1.2 %copy-start = (bf16[128,4096]{1,0:T(8,128)(2,1)S(1)}, bf16[128,4096]{1,0:T(8,128)(2,1)}, u32[]{:S(2)}) copy-start(bf16[128,4096]{1,0:T(8,128)(2,1)} %c_ref.5) | copy-start | bytes 3145732
  5.9 1.5 %copy-start.1 = (bf16[128,4096]{1,0:T(8,128)(2,1)S(1)}, bf16[128,4096]{1,0:T(8,128)(2,1)}, u32[]{:S(2)}) copy-start(bf16[128,4096]{1,0:T(8,128)(2,1)} %q_ref.5) | copy-start | bytes 3145732
  5.9 1.5 %copy-start.2 = (bf16[128,512]{1,0:T(8,128)(2,1)S(1)}, bf16[128,512]{1,0:T(8,128)(2,1)}, u32[]{:S(2)}) copy-start(bf16[128,512]{1,0:T(8,128)(2,1)} %k_ref.3) | copy-start | bytes 393220
  6.0 1.6 %copy-start.3 = (bf16[128,512]{1,0:T(8,128)(2,1)S(1)}, bf16[128,512]{1,0:T(8,128)(2,1)}, u32[]{:S(2)}) copy-start(bf16[128,512]{1,0:T(8,128)(2,1)} %v_ref.1) | copy-start | bytes 393220
  14.7 5.1 %collective-permute-start.3 = (f32[36,128]{1,0:T(8,128)S(1)}, f32[36,128]{1,0:T(8,128)S(1)}, u32[]{:S(2)}, u32[]{:S(2)}) collective-permute-start(f32[36,128]{1,0:T(8,128)S(1)} %get-tuple-element.23), channel_id=1, source_target_pairs={{0,12},{1,13},{2,14},{3,15},{4,8},{5,9},{6,10},{7,11},{8,4},{9,5},... | collective-permute-start | bytes 55304 | tf_op jit(solution)/shard_map/ppermute | solution.py:216
  15.2 4.5 %collective-permute-start.4 = (f32[36,128]{1,0:T(8,128)S(1)}, f32[36,128]{1,0:T(8,128)S(1)}, u32[]{:S(2)}, u32[]{:S(2)}) collective-permute-start(f32[36,128]{1,0:T(8,128)S(1)} %get-tuple-element.23), channel_id=1, source_target_pairs={{0,8},{1,9},{2,10},{3,11},{4,12},{5,13},{6,14},{7,15},{8,0},{9,1},... | collective-permute-start | bytes 55304 | tf_op jit(solution)/shard_map/ppermute | solution.py:216
  16.1 3.7 %collective-permute-start.2 = (f32[36,128]{1,0:T(8,128)S(1)}, f32[36,128]{1,0:T(8,128)S(1)}, u32[]{:S(2)}, u32[]{:S(2)}) collective-permute-start(f32[36,128]{1,0:T(8,128)S(1)} %get-tuple-element.23), channel_id=1, source_target_pairs={{0,4},{1,5},{2,6},{3,7},{4,0},{5,1},{6,2},{7,3},{8,12},{9,13},{10,... | collective-permute-start | bytes 55304 | tf_op jit(solution)/shard_map/ppermute | solution.py:216
  17.5 10.9 %collective-permute-start.9 = (bf16[128,1024]{1,0:T(8,128)(2,1)S(1)}, bf16[128,1024]{1,0:T(8,128)(2,1)S(1)}, u32[]{:S(2)}, u32[]{:S(2)}) collective-permute-start(bf16[128,1024]{1,0:T(8,128)(2,1)S(1)} %get-tuple-element.27), channel_id=1, source_target_pairs={{0,31},{1,0},{2,1},{3,2},{4,3},{5,4},{6,5},{7,6},{8,7},{9,8},{10,9... | collective-permute-start | bytes 786440 | tf_op jit(solution)/shard_map/ppermute | solution.py:197
  19.8 3.3 %collective-permute-start.5 = (f32[36,128]{1,0:T(8,128)S(1)}, f32[36,128]{1,0:T(8,128)S(1)}, u32[]{:S(2)}, u32[]{:S(2)}) collective-permute-start(f32[36,128]{1,0:T(8,128)S(1)} %add_add_fusion.refs_0_), channel_id=1, source_target_pairs={{0,20},{1,21},{2,22},{3,23},{4,16},{5,17},{6,18},{7,19},{8,28},{9,... | collective-permute-start | bytes 55304 | tf_op jit(solution)/shard_map/ppermute | solution.py:216
  23.0 3.4 %collective-permute-start.6 = (f32[36,128]{1,0:T(8,128)S(1)}, f32[36,128]{1,0:T(8,128)S(1)}, u32[]{:S(2)}, u32[]{:S(2)}) collective-permute-start(f32[36,128]{1,0:T(8,128)S(1)} %shard_map.88.refs_0_), channel_id=1, source_target_pairs={{0,5},{1,4},{2,7},{3,6},{4,1},{5,0},{6,3},{7,2},{8,13},{9,12},{10,... | collective-permute-start | bytes 55304 | tf_op jit(solution)/shard_map/ppermute | solution.py:216
  23.4 4.2 %collective-permute-start.7 = (f32[36,128]{1,0:T(8,128)S(1)}, f32[36,128]{1,0:T(8,128)S(1)}, u32[]{:S(2)}, u32[]{:S(2)}) collective-permute-start(f32[36,128]{1,0:T(8,128)S(1)} %shard_map.88.refs_0_), channel_id=1, source_target_pairs={{0,6},{1,7},{2,4},{3,5},{4,2},{5,3},{6,0},{7,1},{8,14},{9,15},{10,... | collective-permute-start | bytes 55304 | tf_op jit(solution)/shard_map/ppermute | solution.py:216
  23.4 5.0 %collective-permute-start.8 = (f32[36,128]{1,0:T(8,128)S(1)}, f32[36,128]{1,0:T(8,128)S(1)}, u32[]{:S(2)}, u32[]{:S(2)}) collective-permute-start(f32[36,128]{1,0:T(8,128)S(1)} %shard_map.88.refs_0_), channel_id=1, source_target_pairs={{0,7},{1,6},{2,5},{3,4},{4,3},{5,2},{6,1},{7,0},{8,15},{9,14},{10,... | collective-permute-start | bytes 55304 | tf_op jit(solution)/shard_map/ppermute | solution.py:216

commit v6 on v5

--- a/solution.py
+++ b/solution.py
@@ -69,10 +69,10 @@
     rows = q_ref.shape[0]
     wide = 2 * rows
     spill = spill_of(start_ref[...])
-    taken = lax.broadcasted_iota(jnp.int32, (2 * Q_HEADS, rows), 0)
-    taken = taken - jnp.where(lax.broadcasted_iota(jnp.int32, (2 * Q_HEADS, rows), 1) < spill, 0, Q_HEADS)
+    taken = lax.broadcasted_iota(jnp.int32, (rows, 4 * Q_HEADS), 1)
+    taken = taken - jnp.where(lax.broadcasted_iota(jnp.int32, (rows, 4 * Q_HEADS), 0) < spill, 0, Q_HEADS)
     for h in range(Q_HEADS):
-        pick_ref[:, h * rows : (h + 1) * rows] = jnp.where(taken == h, 1.0, 0.0).astype(jnp.bfloat16)
+        pick_ref[h * rows : (h + 1) * rows, :] = jnp.where(taken == h, 1.0, 0.0).astype(jnp.bfloat16)
     key_row, near = grids(rows, wide)
     start = jnp.concatenate([start_ref[...]] * 2, axis=1)
     far = jnp.logical_not(near) & (key_row - reach * rows >= start)
@@ -115,8 +115,8 @@
             delta = sum(jnp.sum(p_ref[c, at] * d, axis=0, keepdims=True) for d, c in zip(d_parts, cut))
             for d, c in zip(d_parts, cut):
                 g_ref[c, at] = (p_ref[c, at] * (d - delta)).astype(jnp.bfloat16)
-    total = dot(pick_ref[...], g_ref[...], NT) * SCALE
-    early, late = total[:Q_HEADS], total[Q_HEADS:]
+    total = (dot(g_ref[...], pick_ref[...], NN) * SCALE).T
+    early, late = total[:Q_HEADS], total[Q_HEADS : 2 * Q_HEADS]
     spilled = lax.broadcasted_iota(jnp.int32, (Q_HEADS, rows), 1) < spill_of(start_ref[...])
     own_sums = (late[:, :rows] + jnp.where(spilled, early[:, :rows], 0.0)).astype(jnp.bfloat16)
     far_sums = [jnp.where(spilled, 0.0, early[:, :rows]).astype(jnp.bfloat16)]
@@ -175,7 +175,7 @@
     wide_probs, probs, pick = call(
         functools.partial(prob_kernel, reach),
         (start, query, near_s, *far[::2]),
-        [(slots, jnp.float32), (slots, jnp.bfloat16), ((2 * Q_HEADS, Q_HEADS * rows), jnp.bfloat16)],
+        [(slots, jnp.float32), (slots, jnp.bfloat16), ((Q_HEADS * rows, 4 * Q_HEADS), jnp.bfloat16)],
         reach * unit,
     )
     bias, grads = call(

time: 29.4 us -> 29.4 us (level)
  no operation moved by 1% of the time
where the time goes in v6:
time: 29.4 us; the launch traced here: 29.1 us
  starting transfers between devices  12.4 us (42%)
  waiting for transfers between devices  8.63 us (29%)
  Pallas kernels  5.2 us (18%)
  local copies, waits for them, and re-layouts  2.11 us (7%)
  between operations  0.75 us (3%)
    ppermute x3, starting transfers between devices, shift(): lax.ppermute(array, AXES, [(i, (i + by) % count) for i in range(count)])  6.86 us
    ppermute x7, starting transfers between devices, exchange(): lax.ppermute(array, AXES, [(i, i ^ mask) for i in range(count)])  5.53 us
    ppermute x7, waiting for transfers between devices, exchange(): lax.ppermute(array, AXES, [(i, i ^ mask) for i in range(count)])  5.02 us
    pallas_call x6, Pallas kernels, call(): pl.pallas_call(kernel, out_shape=[jax.ShapeDtypeStruct(*out) for out in o...  4.43 us
    ppermute x3, waiting for transfers between devices, shift(): lax.ppermute(array, AXES, [(i, (i + by) % count) for i in range(count)])  3.61 us
    unnamed x10, local copies, waits for them, and re-layouts  2.11 us
    pallas_call x1, Pallas kernels, last(): pl.pallas_call(functools.partial(last_kernel, len(terms), len(parts)), ou...  0.77 us
  transfers between devices with their start and end apart: 10, of which 5 were waited for; matrix products, arithmetic and copies ran while one was open for 0% of the time, Pallas kernels for 11%

profile of v6, /device:TPU:0, one launch (start us, length us, event | category | flops | bytes accessed | tf_op | source)
XLA Modules:
  0.0 29.1 jit_solution(13157539854694364614)
XLA Ops:
  0.6 3.1 %collective-permute-start = (bf16[128,512]{1,0:T(8,128)(2,1)}, bf16[128,512]{1,0:T(8,128)(2,1)S(1)}, u32[]{:S(2)}, u32[]{:S(2)}) collective-permute-start(bf16[128,512]{1,0:T(8,128)(2,1)} %k_ref.3), channel_id=1, source_target_pairs={{0,1},{1,2},{2,3},{3,4},{4,5},{5,6},{6,7},{7,8},{8,9},{9,10},{10,1... | collective-permute-start | bytes 393224 | tf_op jit(solution)/shard_map/ppermute | solution.py:197
  3.7 1.6 %collective-permute-start.1 = (bf16[128,512]{1,0:T(8,128)(2,1)}, bf16[128,512]{1,0:T(8,128)(2,1)S(1)}, u32[]{:S(2)}, u32[]{:S(2)}) collective-permute-start(bf16[128,512]{1,0:T(8,128)(2,1)} %v_ref.1), channel_id=1, source_target_pairs={{0,1},{1,2},{2,3},{3,4},{4,5},{5,6},{6,7},{7,8},{8,9},{9,10},{10,1... | collective-permute-start | bytes 393224 | tf_op jit(solution)/shard_map/ppermute | solution.py:197
  5.3 0.0 copy-start.4
  5.3 0.7 %copy-done.4 = s32[64]{0:T(128)S(1)} copy-done((s32[64]{0:T(128)S(1)}, s32[64]{0:T(128)}, u32[]{:S(2)}) %copy-start.4) | copy-done | bytes 280
  6.0 0.1 shard_map.84.start_ref
  6.1 1.1 %copy-done = bf16[128,4096]{1,0:T(8,128)(2,1)S(1)} copy-done((bf16[128,4096]{1,0:T(8,128)(2,1)S(1)}, bf16[128,4096]{1,0:T(8,128)(2,1)}, u32[]{:S(2)}) %copy-start) | copy-done | bytes 1048600
  7.2 0.3 %copy-done.1 = bf16[128,4096]{1,0:T(8,128)(2,1)S(1)} copy-done((bf16[128,4096]{1,0:T(8,128)(2,1)S(1)}, bf16[128,4096]{1,0:T(8,128)(2,1)}, u32[]{:S(2)}) %copy-start.1) | copy-done | bytes 1048600
  7.5 0.0 copy-done.2
  7.5 0.0 copy-done.3
  7.5 0.8 %shard_map.85 = (f32[128,4096]{1,0:T(8,128)S(1)}, f32[128,4096]{1,0:T(8,128)S(1)}, f32[8,128]{1,0:T(8,128)S(1)}) custom-call(s32[1,128]{1,0:T(1,128)S(1)} %shard_map.84.start_ref, bf16[128,4096]{1,0:T(8,128)(2,1)S(1)} %copy-done.1, bf16[128,4096]{1,0:T(8,128)(2,1)S(1)} %copy-done, bf16[128,512]{1,0:T(8,128)(2,1)S(1)} %copy-done.2, bf16[128,512]{1,0:T(8,128)(2,1)S(1)} %copy-done.3), custom_call_target="tpu_custom_call" | custom-call | flops 268435456 | bytes 2097152 | tf_op jit(solution)/shard_map/pallas_call | solution.py:154
  8.3 2.2 %collective-permute-done.refs_0_ = bf16[128,512]{1,0:T(8,128)(2,1)S(1)} collective-permute-done((bf16[128,512]{1,0:T(8,128)(2,1)}, bf16[128,512]{1,0:T(8,128)(2,1)S(1)}, u32[]{:S(2)}, u32[]{:S(2)}) %collective-permute-start) | collective-permute-done | bytes 131104 | tf_op jit(solution)/shard_map/ppermute | solution.py:197
  10.5 1.4 %shard_map.86 = (f32[128,4096]{1,0:T(8,128)S(1)}, bf16[128,4096]{1,0:T(8,128)(2,1)S(1)}, bf16[4096,128]{1,0:T(8,128)(2,1)S(1)}) custom-call(s32[1,128]{1,0:T(1,128)S(1)} %shard_map.84.start_ref, bf16[128,4096]{1,0:T(8,128)(2,1)S(1)} %copy-done.1, f32[128,4096]{1,0:T(8,128)S(1)} %get-tuple-element.20.s_ref, bf16[128,512]{1,0:T(8,128)(2,1)S(1)} %collective-permute-done.refs_0_), custom_call_target="tpu_custom_call" | custom-call | flops 134217728 | bytes 2097152 | tf_op jit(solution)/shard_map/pallas_call | solution.py:154
  11.9 1.5 %collective-permute-done.1.refs_1_ = bf16[128,512]{1,0:T(8,128)(2,1)S(1)} collective-permute-done((bf16[128,512]{1,0:T(8,128)(2,1)}, bf16[128,512]{1,0:T(8,128)(2,1)S(1)}, u32[]{:S(2)}, u32[]{:S(2)}) %collective-permute-start.1) | collective-permute-done | bytes 131104 | tf_op jit(solution)/shard_map/ppermute | solution.py:197
  13.3 1.2 %shard_map.87 = (f32[36,128]{1,0:T(8,128)S(1)}, bf16[128,4096]{1,0:T(8,128)(2,1)S(1)}) custom-call(s32[1,128]{1,0:T(1,128)S(1)} %shard_map.84.start_ref, bf16[128,512]{1,0:T(8,128)(2,1)S(1)} %copy-done.2, bf16[128,4096]{1,0:T(8,128)(2,1)S(1)} %copy-done, f32[128,4096]{1,0:T(8,128)S(1)} %get-tuple-element.18.d_ref, f32[8,128]{1,0:T(8,128)S(1)} %get-tuple-element.19.sum_ref, ...), custom_call_target="tpu_custom_call" | custom-call | flops 268435456 | bytes 2097152 | tf_op jit(solution)/shard_map/pallas_call | solution.py:154
  14.6 0.5 %collective-permute-start.3 = (f32[36,128]{1,0:T(8,128)S(1)}, f32[36,128]{1,0:T(8,128)S(1)}, u32[]{:S(2)}, u32[]{:S(2)}) collective-permute-start(f32[36,128]{1,0:T(8,128)S(1)} %get-tuple-element.23), channel_id=1, source_target_pairs={{0,12},{1,13},{2,14},{3,15},{4,8},{5,9},{6,10},{7,11},{8,4},{9,5},... | collective-permute-start | bytes 55304 | tf_op jit(solution)/shard_map/ppermute | solution.py:216
  15.2 0.8 %collective-permute-start.4 = (f32[36,128]{1,0:T(8,128)S(1)}, f32[36,128]{1,0:T(8,128)S(1)}, u32[]{:S(2)}, u32[]{:S(2)}) collective-permute-start(f32[36,128]{1,0:T(8,128)S(1)} %get-tuple-element.23), channel_id=1, source_target_pairs={{0,8},{1,9},{2,10},{3,11},{4,12},{5,13},{6,14},{7,15},{8,0},{9,1},... | collective-permute-start | bytes 55304 | tf_op jit(solution)/shard_map/ppermute | solution.py:216
  16.0 0.5 %collective-permute-start.2 = (f32[36,128]{1,0:T(8,128)S(1)}, f32[36,128]{1,0:T(8,128)S(1)}, u32[]{:S(2)}, u32[]{:S(2)}) collective-permute-start(f32[36,128]{1,0:T(8,128)S(1)} %get-tuple-element.23), channel_id=1, source_target_pairs={{0,4},{1,5},{2,6},{3,7},{4,0},{5,1},{6,2},{7,3},{8,12},{9,13},{10,... | collective-permute-start | bytes 55304 | tf_op jit(solution)/shard_map/ppermute | solution.py:216
  16.5 0.9 %shard_map.89 = (bf16[128,1024]{1,0:T(8,128)(2,1)S(1)}, bf16[128,1024]{1,0:T(8,128)(2,1)S(1)}) custom-call(s32[1,128]{1,0:T(1,128)S(1)} %shard_map.84.start_ref, bf16[128,4096]{1,0:T(8,128)(2,1)S(1)} %copy-done.1, bf16[128,4096]{1,0:T(8,128)(2,1)S(1)} %copy-done, bf16[128,4096]{1,0:T(8,128)(2,1)S(1)} %get-tuple-element.24.p_ref, ...), custom_call_target="tpu_custom_call" | custom-call | flops 268435456 | bytes 2097152 | tf_op jit(solution)/shard_map/pallas_call | solution.py:154
  17.5 2.2 %collective-permute-start.9 = (bf16[128,1024]{1,0:T(8,128)(2,1)S(1)}, bf16[128,1024]{1,0:T(8,128)(2,1)S(1)}, u32[]{:S(2)}, u32[]{:S(2)}) collective-permute-start(bf16[128,1024]{1,0:T(8,128)(2,1)S(1)} %get-tuple-element.27), channel_id=1, source_target_pairs={{0,31},{1,0},{2,1},{3,2},{4,3},{5,4},{6,5},{7,6},{8,7},{9,8},{10,9... | collective-permute-start | bytes 786440 | tf_op jit(solution)/shard_map/ppermute | solution.py:197
  19.7 0.0 collective-permute-done.3
  19.7 0.0 collective-permute-done.4
  19.7 0.0 collective-permute-done.2
  19.7 0.2 collective-permute-start.5
  19.9 3.1 %collective-permute-done.5.refs_1_ = f32[36,128]{1,0:T(8,128)S(1)} collective-permute-done((f32[36,128]{1,0:T(8,128)S(1)}, f32[36,128]{1,0:T(8,128)S(1)}, u32[]{:S(2)}, u32[]{:S(2)}) %collective-permute-start.5) | collective-permute-done | bytes 18464 | tf_op jit(solution)/shard_map/ppermute | solution.py:216
  23.0 0.3 %collective-permute-start.6 = (f32[36,128]{1,0:T(8,128)S(1)}, f32[36,128]{1,0:T(8,128)S(1)}, u32[]{:S(2)}, u32[]{:S(2)}) collective-permute-start(f32[36,128]{1,0:T(8,128)S(1)} %shard_map.88.refs_0_), channel_id=1, source_target_pairs={{0,5},{1,4},{2,7},{3,6},{4,1},{5,0},{6,3},{7,2},{8,13},{9,12},{10,... | collective-permute-start | bytes 55304 | tf_op jit(solution)/shard_map/ppermute | solution.py:216
  23.3 0.0 collective-permute-start.7
  23.3 3.1 %collective-permute-start.8 = (f32[36,128]{1,0:T(8,128)S(1)}, f32[36,128]{1,0:T(8,128)S(1)}, u32[]{:S(2)}, u32[]{:S(2)}) collective-permute-start(f32[36,128]{1,0:T(8,128)S(1)} %shard_map.88.refs_0_), channel_id=1, source_target_pairs={{0,7},{1,6},{2,5},{3,4},{4,3},{5,2},{6,1},{7,0},{8,15},{9,14},{10,... | collective-permute-start | bytes 55304 | tf_op jit(solution)/shard_map/ppermute | solution.py:216
  26.4 0.0 collective-permute-done.6.refs_1_
  26.4 1.1 %collective-permute-done.7.refs_2_ = f32[36,128]{1,0:T(8,128)S(1)} collective-permute-done((f32[36,128]{1,0:T(8,128)S(1)}, f32[36,128]{1,0:T(8,128)S(1)}, u32[]{:S(2)}, u32[]{:S(2)}) %collective-permute-start.7) | collective-permute-done | bytes 18464 | tf_op jit(solution)/shard_map/ppermute | solution.py:216
  27.5 0.8 %collective-permute-done.8.refs_3_ = f32[36,128]{1,0:T(8,128)S(1)} collective-permute-done((f32[36,128]{1,0:T(8,128)S(1)}, f32[36,128]{1,0:T(8,128)S(1)}, u32[]{:S(2)}, u32[]{:S(2)}) %collective-permute-start.8) | collective-permute-done | bytes 18464 | tf_op jit(solution)/shard_map/ppermute | solution.py:216
  28.3 0.0 collective-permute-done.9.refs_5_
  28.3 0.8 %shard_map.90 = (f32[32,128]{1,0:T(8,128)}, f32[4,128]{1,0:T(4,128)}, bf16[128,512]{1,0:T(8,128)(2,1)}, bf16[128,512]{1,0:T(8,128)(2,1)}) custom-call(f32[36,128]{1,0:T(8,128)S(1)} %shard_map.88.refs_0_, f32[36,128]{1,0:T(8,128)S(1)} %collective-permute-done.6.refs_1_, f32[36,128]{1,0:T(8,128)S(1)} %collective-permute-done.7.refs_2_, ...), custom_call_target="tpu_custom_call" | custom-call | tf_op jit(solution)/shard_map/pallas_call | solution.py:257
  (6 shorter events, 0.0 us)
Async XLA Ops:
  0.6 9.9 %collective-permute-start = (bf16[128,512]{1,0:T(8,128)(2,1)}, bf16[128,512]{1,0:T(8,128)(2,1)S(1)}, u32[]{:S(2)}, u32[]{:S(2)}) collective-permute-start(bf16[128,512]{1,0:T(8,128)(2,1)} %k_ref.3), channel_id=1, source_target_pairs={{0,1},{1,2},{2,3},{3,4},{4,5},{5,6},{6,7},{7,8},{8,9},{9,10},{10,1... | collective-permute-start | bytes 393224 | tf_op jit(solution)/shard_map/ppermute | solution.py:197
  3.7 9.6 %collective-permute-start.1 = (bf16[128,512]{1,0:T(8,128)(2,1)}, bf16[128,512]{1,0:T(8,128)(2,1)S(1)}, u32[]{:S(2)}, u32[]{:S(2)}) collective-permute-start(bf16[128,512]{1,0:T(8,128)(2,1)} %v_ref.1), channel_id=1, source_target_pairs={{0,1},{1,2},{2,3},{3,4},{4,5},{5,6},{6,7},{7,8},{8,9},{9,10},{10,1... | collective-permute-start | bytes 393224 | tf_op jit(solution)/shard_map/ppermute | solution.py:197
  5.3 0.7 %copy-start.4 = (s32[64]{0:T(128)S(1)}, s32[64]{0:T(128)}, u32[]{:S(2)}) copy-start(s32[64]{0:T(128)} %param.9) | copy-start | bytes 772
  5.9 1.2 %copy-start = (bf16[128,4096]{1,0:T(8,128)(2,1)S(1)}, bf16[128,4096]{1,0:T(8,128)(2,1)}, u32[]{:S(2)}) copy-start(bf16[128,4096]{1,0:T(8,128)(2,1)} %c_ref.5) | copy-start | bytes 3145732
  5.9 1.5 %copy-start.1 = (bf16[128,4096]{1,0:T(8,128)(2,1)S(1)}, bf16[128,4096]{1,0:T(8,128)(2,1)}, u32[]{:S(2)}) copy-start(bf16[128,4096]{1,0:T(8,128)(2,1)} %q_ref.5) | copy-start | bytes 3145732
  5.9 1.5 %copy-start.2 = (bf16[128,512]{1,0:T(8,128)(2,1)S(1)}, bf16[128,512]{1,0:T(8,128)(2,1)}, u32[]{:S(2)}) copy-start(bf16[128,512]{1,0:T(8,128)(2,1)} %k_ref.3) | copy-start | bytes 393220
  6.0 1.6 %copy-start.3 = (bf16[128,512]{1,0:T(8,128)(2,1)S(1)}, bf16[128,512]{1,0:T(8,128)(2,1)}, u32[]{:S(2)}) copy-start(bf16[128,512]{1,0:T(8,128)(2,1)} %v_ref.1) | copy-start | bytes 393220
  14.6 5.1 %collective-permute-start.3 = (f32[36,128]{1,0:T(8,128)S(1)}, f32[36,128]{1,0:T(8,128)S(1)}, u32[]{:S(2)}, u32[]{:S(2)}) collective-permute-start(f32[36,128]{1,0:T(8,128)S(1)} %get-tuple-element.23), channel_id=1, source_target_pairs={{0,12},{1,13},{2,14},{3,15},{4,8},{5,9},{6,10},{7,11},{8,4},{9,5},... | collective-permute-start | bytes 55304 | tf_op jit(solution)/shard_map/ppermute | solution.py:216
  15.2 4.5 %collective-permute-start.4 = (f32[36,128]{1,0:T(8,128)S(1)}, f32[36,128]{1,0:T(8,128)S(1)}, u32[]{:S(2)}, u32[]{:S(2)}) collective-permute-start(f32[36,128]{1,0:T(8,128)S(1)} %get-tuple-element.23), channel_id=1, source_target_pairs={{0,8},{1,9},{2,10},{3,11},{4,12},{5,13},{6,14},{7,15},{8,0},{9,1},... | collective-permute-start | bytes 55304 | tf_op jit(solution)/shard_map/ppermute | solution.py:216
  16.0 3.7 %collective-permute-start.2 = (f32[36,128]{1,0:T(8,128)S(1)}, f32[36,128]{1,0:T(8,128)S(1)}, u32[]{:S(2)}, u32[]{:S(2)}) collective-permute-start(f32[36,128]{1,0:T(8,128)S(1)} %get-tuple-element.23), channel_id=1, source_target_pairs={{0,4},{1,5},{2,6},{3,7},{4,0},{5,1},{6,2},{7,3},{8,12},{9,13},{10,... | collective-permute-start | bytes 55304 | tf_op jit(solution)/shard_map/ppermute | solution.py:216
  17.5 10.9 %collective-permute-start.9 = (bf16[128,1024]{1,0:T(8,128)(2,1)S(1)}, bf16[128,1024]{1,0:T(8,128)(2,1)S(1)}, u32[]{:S(2)}, u32[]{:S(2)}) collective-permute-start(bf16[128,1024]{1,0:T(8,128)(2,1)S(1)} %get-tuple-element.27), channel_id=1, source_target_pairs={{0,31},{1,0},{2,1},{3,2},{4,3},{5,4},{6,5},{7,6},{8,7},{9,8},{10,9... | collective-permute-start | bytes 786440 | tf_op jit(solution)/shard_map/ppermute | solution.py:197
  19.7 3.3 %collective-permute-start.5 = (f32[36,128]{1,0:T(8,128)S(1)}, f32[36,128]{1,0:T(8,128)S(1)}, u32[]{:S(2)}, u32[]{:S(2)}) collective-permute-start(f32[36,128]{1,0:T(8,128)S(1)} %add_add_fusion.refs_0_), channel_id=1, source_target_pairs={{0,20},{1,21},{2,22},{3,23},{4,16},{5,17},{6,18},{7,19},{8,28},{9,... | collective-permute-start | bytes 55304 | tf_op jit(solution)/shard_map/ppermute | solution.py:216
  23.0 3.4 %collective-permute-start.6 = (f32[36,128]{1,0:T(8,128)S(1)}, f32[36,128]{1,0:T(8,128)S(1)}, u32[]{:S(2)}, u32[]{:S(2)}) collective-permute-start(f32[36,128]{1,0:T(8,128)S(1)} %shard_map.88.refs_0_), channel_id=1, source_target_pairs={{0,5},{1,4},{2,7},{3,6},{4,1},{5,0},{6,3},{7,2},{8,13},{9,12},{10,... | collective-permute-start | bytes 55304 | tf_op jit(solution)/shard_map/ppermute | solution.py:216
  23.3 4.2 %collective-permute-start.7 = (f32[36,128]{1,0:T(8,128)S(1)}, f32[36,128]{1,0:T(8,128)S(1)}, u32[]{:S(2)}, u32[]{:S(2)}) collective-permute-start(f32[36,128]{1,0:T(8,128)S(1)} %shard_map.88.refs_0_), channel_id=1, source_target_pairs={{0,6},{1,7},{2,4},{3,5},{4,2},{5,3},{6,0},{7,1},{8,14},{9,15},{10,... | collective-permute-start | bytes 55304 | tf_op jit(solution)/shard_map/ppermute | solution.py:216
  23.3 5.0 %collective-permute-start.8 = (f32[36,128]{1,0:T(8,128)S(1)}, f32[36,128]{1,0:T(8,128)S(1)}, u32[]{:S(2)}, u32[]{:S(2)}) collective-permute-start(f32[36,128]{1,0:T(8,128)S(1)} %shard_map.88.refs_0_), channel_id=1, source_target_pairs={{0,7},{1,6},{2,5},{3,4},{4,3},{5,2},{6,1},{7,0},{8,15},{9,14},{10,... | collective-permute-start | bytes 55304 | tf_op jit(solution)/shard_map/ppermute | solution.py:216
